TPU v7x, 32 devices: a whole 2x2x4 slice. The times are simulated.
32 devices in a mesh: dom: 32 (over z, y, x, core).
Axes of the slice: x: 2, y: 2, z: 4, core: 2. Of those that a mesh axis runs over, the one named last changes fastest.
Arguments:
- connectivity: int32 [4096, 64], P('dom'), may hold values from 0 to 4991, as said below
- send_down: int32 [32, 768], P('dom'), may hold values from 0 to 3455, as said below
- send_up: int32 [32, 768], P('dom'), may hold values from 0 to 3455, as said below
- jacobian: float32 [4096], P('dom'), may hold values from 0.5 to 4
- pair_blocks: bfloat16 [8192, 4096], P('dom'), may hold values from -0.75 to 0.75
- pair_target: int32 [8192], P('dom'), may hold values from 0 to 127
- pair_source: int32 [8192], P('dom'), may hold values from 0 to 127
- source_values: bfloat16 [32, 262144], P(None, 'dom'), may hold values from -6 to 6
Outputs:
- solution: float32 [32, 110592], P(None, 'dom')
- residual: float32 [32, 110592], P(None, 'dom')
- new_basis: float32 [32, 110592], P(None, 'dom')
Inputs may be any that keep to these rules, and one draw needn't show every extreme that they name: `connectivity`: slots below 3456 are the partition's own nodes, the next 768 the lower neighbour's send_up list in order, the last 768 the upper neighbour's send_down list in order; the first partition uses no lower slots, the last no upper ones. `send_down`: distinct own node indices in each row. `send_up`: distinct own node indices in each row.
All inputs are finite; a program needn't handle non-finite values.
Results may differ from a plain program's by a relative error of at most 0.0003.
Values sent between devices are 32-bit elements; how exact they have to be, the bound alone decides.
A program may use at most 64 MiB of HBM per device.

v0:
```python
import jax
import jax.numpy as jnp
import numpy as np
from jax import lax
from jax.sharding import PartitionSpec as P

NP = 64
NODE_DEV = 3456
F = 768


line_mass = (
    np.array(
        [
            [128.0, 99.0, -36.0, 19.0],
            [99.0, 648.0, -81.0, -36.0],
            [-36.0, -81.0, 648.0, 99.0],
            [19.0, -36.0, 99.0, 128.0],
        ]
    )
    / 504.0
)
mass_table = np.kron(np.kron(line_mass, line_mass), line_mass)


def shifted(value, axis, by):
    size = lax.axis_size(axis)
    pairs = [(i, i + by) for i in range(size) if 0 <= i + by < size]
    return lax.ppermute(value, axis, pairs)


def per_device(
    connectivity, send_down, send_up, jacobian, pair_blocks, pair_target, pair_source, source_values
):
    high = lax.Precision.HIGHEST
    tracers = source_values.shape[0]
    owned = NODE_DEV
    lows = send_down[0]
    highs = send_up[0]
    elements = connectivity.shape[0]
    pairs = pair_target.shape[0]
    flat_ids = connectivity.reshape(-1)
    element_mass = jnp.asarray(mass_table, dtype=jnp.float32)

    def spread(values, slots):
        return jnp.zeros((tracers, owned + 2 * F), jnp.float32).at[:, slots].add(values)

    def settle(extended):
        own_part = extended[:, :owned]
        from_above = shifted(extended[:, owned : owned + F], "dom", -1)
        from_below = shifted(extended[:, owned + F :], "dom", 1)
        return own_part.at[:, highs].add(from_above).at[:, lows].add(from_below)

    def lower_solve(lower, matrix):
        return jax.scipy.linalg.solve_triangular(lower, matrix, lower=True)

    offsets = jnp.arange(NP, dtype=jnp.int32)
    columns = (pair_source[:, None] * NP + offsets[None, :]).reshape(-1)
    gathered = source_values[:, columns].reshape(tracers, pairs, NP)
    mixed = pair_blocks.reshape(pairs, NP, NP)
    contrib = jnp.einsum("pij,tpj->tpi", mixed, gathered, preferred_element_type=jnp.float32)
    targets = connectivity[pair_target].reshape(-1)
    right_side = settle(spread(contrib.reshape(tracers, pairs * NP), targets))
    rhs_gram_local = jnp.dot(right_side, right_side.T, precision=high)
    sums = lax.psum((rhs_gram_local,), "dom")
    gram_rhs = sums[0]
    lower_rhs = jnp.linalg.cholesky(gram_rhs)
    basis = lower_solve(lower_rhs, right_side)
    below = shifted(basis[:, highs], "dom", 1)
    above = shifted(basis[:, lows], "dom", -1)
    values = jnp.concatenate([basis, below, above], axis=1)[:, flat_ids].reshape(
        tracers, elements, NP
    )
    image = (
        jnp.einsum("tep,pq->teq", values, element_mass, precision=high) * jacobian[None, :, None]
    )
    image = settle(spread(image.reshape(tracers, elements * NP), flat_ids))
    step_gram = lax.psum(jnp.dot(basis, image.T, precision=high), "dom")
    lower_step = jnp.linalg.cholesky(step_gram)
    coeffs = jax.scipy.linalg.cho_solve((lower_step, True), lower_rhs.T).T
    solution = jnp.dot(coeffs, basis, precision=high)
    residual = right_side - jnp.dot(coeffs, image, precision=high)
    gram_new = lax.psum(jnp.dot(residual, residual.T, precision=high), "dom")
    lower_new = jnp.linalg.cholesky(gram_new)
    new_basis = lower_solve(lower_new, residual)
    return (solution, residual, new_basis)


def solution(mesh):
    return jax.shard_map(
        per_device,
        mesh=mesh,
        in_specs=(
            P("dom", None),
            P("dom", None),
            P("dom", None),
            P("dom"),
            P("dom", None),
            P("dom"),
            P("dom"),
            P(None, "dom"),
        ),
        out_specs=(P(None, "dom"), P(None, "dom"), P(None, "dom")),
        check_vma=False,
    )
```

profile of v0, /device:TPU:0, one launch (start us, length us, event | category | flops | bytes accessed | tf_op | source)
XLA Modules:
  0.0 500.2 jit_solution(3358379403600781660)
XLA Ops:
  3.1 1.9 copy.29
  5.4 4.1 copy.30
  9.5 7.5 %copy.32 = bf16[256,64,64]{2,1,0:T(8,128)(2,1)} copy(bf16[256,64,64]{0,2,1:T(8,128)(2,1)} %bitcast.80) | data formatting | bytes 4194304 | tf_op jit(solution)/shard_map/reshape | solution.py:60
  17.0 57.4 %gather_fusion.1 = bf16[16384,32]{1,0:T(8,128)(2,1)} fusion(bf16[32,8192]{0,1:T(8,128)(2,1)S(1)} %copy.29, s32[16384]{0:T(1024)S(1)} %broadcast_clamp_fusion), kind=kCustom, calls=%fused_computation.1 | custom fusion | bytes 2162688 | tf_op jit(solution)/shard_map/gather | solution.py:59
  74.3 5.8 %convolution_bitcast_fusion = f32[32,256,64]{2,0,1:T(8,128)S(1)} fusion(bf16[32,256,64]{0,2,1:T(8,128)(2,1)} %bitcast.81, bf16[256,64,64]{2,1,0:T(8,128)(2,1)} %copy.32), kind=kOutput, calls=%fused_computation.11 | convolution fusion | flops 67108864 | bytes 5242880 | tf_op jit(solution)/shard_map/pij,tpj->tpi/dot_general | solution.py:61
  80.1 4.4 copy.33
  84.5 2.9 reshape.235
  87.4 4.7 copy.34
  92.1 88.3 %scatter_custom_fusion = f32[32,4992]{0,1:T(8,128)S(1)} fusion(s32[16384]{0:T(1024)S(1)} %bitcast.89, f32[16384,32]{1,0:T(8,128)} %copy.34, f32[]{:T(128)} %constant.56.clone.1), kind=kCustom, calls=%fused_computation.15 | custom fusion | flops 524288 | bytes 639488 | tf_op jit(solution)/shard_map/scatter-add | solution.py:46
  180.5 1.4 collective-permute-start
  181.9 3.8 collective-permute-start.1
  185.7 1.6 slice.54
  187.5 7.3 %scatter_custom_fusion.1 = f32[32,3456]{0,1:T(8,128)S(1)} fusion(f32[32,3456]{0,1:T(8,128)S(1)} %slice.54, s32[768]{0:T(1024)S(1)} %fusion.30, f32[32,768]{0,1:T(8,128)} %collective-permute-done), kind=kCustom, calls=%fused_computation.24 | custom fusion | flops 24576 | bytes 540672 | tf_op jit(solution)/shard_map/scatter-add | solution.py:52
  194.9 7.1 %scatter_custom_fusion.2 = f32[32,3456]{0,1:T(8,128)S(1)} fusion(f32[32,3456]{0,1:T(8,128)S(1)} %scatter_custom_fusion.1, s32[768]{0:T(1024)S(1)} %fusion.31, f32[32,768]{0,1:T(8,128)} %collective-permute-done.1), kind=kCustom, calls=%fused_computation.22 | custom fusion | flops 24576 | bytes 540672 | tf_op jit(solution)/shard_map/scatter-add | solution.py:52
  202.0 3.0 fusion.36
  205.0 45.6 %psum.21 = f32[32,32]{0,1:T(8,128)S(1)} all-reduce(f32[32,32]{0,1:T(8,128)S(1)} %fusion.36), channel_id=1, replica_groups=mesh['dom'=32] {'dom'}, use_global_device_ids=true, to_apply=%region_3.0 | all-reduce | flops 1024 | bytes 8192 | tf_op jit(solution)/shard_map/psum | solution.py:65
  250.7 2.9 cholesky.59
  255.0 2.4 custom-call.14
  257.4 2.0 fusion.22
  259.4 1.8 copy.38
  261.1 3.0 gather_fusion.2
  264.3 1.3 collective-permute-start.2
  265.6 3.0 gather_fusion.3
  268.8 1.5 collective-permute-start.3
  270.4 4.2 collective-permute-done.3
  275.4 2.2 copy.42
  277.6 27.7 %gather_fusion.4 = f32[8192,32]{1,0:T(8,128)} fusion(f32[32,4992]{0,1:T(8,128)S(1)} %copy.42, s32[8192]{0:T(1024)S(1)} %broadcast_clamp_fusion.1), kind=kCustom, calls=%fused_computation.4 | custom fusion | bytes 2129920 | tf_op jit(solution)/shard_map/gather | solution.py:71
  305.3 4.1 copy.43
  309.5 2.1 convolution_multiply_fusion
  311.6 1.8 copy.44
  313.4 1.6 reshape.259
  315.0 3.6 copy.45
  318.6 46.0 %scatter_custom_fusion.3 = f32[32,4992]{0,1:T(8,128)} fusion(s32[8192]{0:T(1024)S(1)} %bitcast.86, f32[8192,32]{1,0:T(8,128)} %copy.45, f32[]{:T(128)} %constant.56.clone.1), kind=kCustom, calls=%fused_computation.13 | custom fusion | flops 262144 | bytes 639488 | tf_op jit(solution)/shard_map/scatter-add | solution.py:46
  364.6 1.9 fusion.34
  367.8 6.5 %collective-permute-start.5 = (f32[32,768]{0,1:T(8,128)S(1)}, f32[32,768]{0,1:T(8,128)}, u32[]{:S(2)}, u32[]{:S(2)}) collective-permute-start(f32[32,768]{0,1:T(8,128)S(1)} %get-tuple-element.5), channel_id=1, source_target_pairs={{0,1},{1,2},{2,3},{3,4},{4,5},{5,6},{6,7},{7,8},{8,9},{9,10},{10,1... | collective-permute-start | bytes 294920 | tf_op jit(solution)/shard_map/ppermute | solution.py:29
  374.9 1.5 slice-done
  376.4 7.1 %scatter_custom_fusion.4 = f32[32,3456]{0,1:T(8,128)S(1)} fusion(f32[32,3456]{0,1:T(8,128)S(1)} %slice-done, s32[768]{0:T(1024)S(1)} %fusion.30, f32[32,768]{0,1:T(8,128)} %collective-permute-done.4), kind=kCustom, calls=%fused_computation.20 | custom fusion | flops 24576 | bytes 540672 | tf_op jit(solution)/shard_map/scatter-add | solution.py:52
  383.5 7.4 %scatter_custom_fusion.5 = f32[32,3456]{0,1:T(8,128)S(1)} fusion(f32[32,3456]{0,1:T(8,128)S(1)} %scatter_custom_fusion.4, s32[768]{0:T(1024)S(1)} %fusion.31, f32[32,768]{0,1:T(8,128)} %collective-permute-done.5), kind=kCustom, calls=%fused_computation.18 | custom fusion | flops 24576 | bytes 540672 | tf_op jit(solution)/shard_map/scatter-add | solution.py:52
  390.9 2.9 fusion.37
  393.8 47.2 %psum.22 = f32[32,32]{0,1:T(8,128)S(1)} all-reduce(f32[32,32]{0,1:T(8,128)S(1)} %fusion.37), channel_id=1, replica_groups=mesh['dom'=32] {'dom'}, use_global_device_ids=true, to_apply=%region_9.12 | all-reduce | flops 1024 | bytes 8192 | tf_op jit(solution)/shard_map/psum | solution.py:78
  441.0 2.9 cholesky.70
  445.3 2.4 custom-call.12
  448.7 2.0 fusion.39
  450.7 1.3 fusion.38
  452.6 39.1 %psum.23 = f32[32,32]{0,1:T(8,128)S(1)} all-reduce(f32[32,32]{0,1:T(8,128)S(1)} %fusion.40), channel_id=1, replica_groups=mesh['dom'=32] {'dom'}, use_global_device_ids=true, to_apply=%region_10.13 | all-reduce | flops 1024 | bytes 8192 | tf_op jit(solution)/shard_map/psum | solution.py:83
  491.7 2.9 cholesky.81
  496.0 2.4 custom-call.15
  498.4 1.4 fusion.14
  (67 shorter events, 11.8 us)
Async XLA Ops:
  0.6 4.4 copy-start.7
  180.4 1.5 copy-start.2
  180.4 7.0 %copy-start.5 = (s32[1,768]{1,0:T(1,128)S(1)}, s32[1,768]{1,0:T(1,128)}, u32[]{:S(2)}) copy-start(s32[1,768]{1,0:T(1,128)} %param.14) | copy-start | bytes 9220
  180.4 7.0 %copy-start.6 = (s32[1,768]{1,0:T(1,128)S(1)}, s32[1,768]{1,0:T(1,128)}, u32[]{:S(2)}) copy-start(s32[1,768]{1,0:T(1,128)} %param.13) | copy-start | bytes 9220
  180.5 7.1 %collective-permute-start = (f32[32,768]{0,1:T(8,128)S(1)}, f32[32,768]{0,1:T(8,128)}, u32[]{:S(2)}, u32[]{:S(2)}) collective-permute-start(f32[32,768]{0,1:T(8,128)S(1)} %get-tuple-element.8), channel_id=1, source_target_pairs={{1,0},{2,1},{3,2},{4,3},{5,4},{6,5},{7,6},{8,7},{9,8},{10,9},{11,1... | collective-permute-start | bytes 294920 | tf_op jit(solution)/shard_map/ppermute | solution.py:29
  181.9 13.0 %collective-permute-start.1 = (f32[32,768]{0,1:T(8,128)S(1)}, f32[32,768]{0,1:T(8,128)}, u32[]{:S(2)}, u32[]{:S(2)}) collective-permute-start(f32[32,768]{0,1:T(8,128)S(1)} %get-tuple-element.7), channel_id=1, source_target_pairs={{0,1},{1,2},{2,3},{3,4},{4,5},{5,6},{6,7},{7,8},{8,9},{9,10},{10,1... | collective-permute-start | bytes 294920 | tf_op jit(solution)/shard_map/ppermute | solution.py:29
  202.0 57.4 %copy-start = (f32[32,3456]{0,1:T(8,128)}, f32[32,3456]{0,1:T(8,128)S(1)}, u32[]{:S(2)}) copy-start(f32[32,3456]{0,1:T(8,128)S(1)} %scatter_custom_fusion.2) | copy-start | bytes 1327108
  264.3 6.0 %collective-permute-start.2 = (f32[32,768]{1,0:T(8,128)S(1)}, f32[32,768]{1,0:T(8,128)S(1)}, u32[]{:S(2)}, u32[]{:S(2)}) collective-permute-start(f32[32,768]{1,0:T(8,128)S(1)} %bitcast.87), channel_id=1, source_target_pairs={{0,1},{1,2},{2,3},{3,4},{4,5},{5,6},{6,7},{7,8},{8,9},{9,10},{10,1... | collective-permute-start | bytes 294920 | tf_op jit(solution)/shard_map/ppermute | solution.py:29
  268.8 5.7 %collective-permute-start.3 = (f32[32,768]{1,0:T(8,128)S(1)}, f32[32,768]{1,0:T(8,128)S(1)}, u32[]{:S(2)}, u32[]{:S(2)}) collective-permute-start(f32[32,768]{1,0:T(8,128)S(1)} %bitcast.88), channel_id=1, source_target_pairs={{1,0},{2,1},{3,2},{4,3},{5,4},{6,5},{7,6},{8,7},{9,8},{10,9},{11,1... | collective-permute-start | bytes 294920 | tf_op jit(solution)/shard_map/ppermute | solution.py:29
  305.3 4.1 copy-start.4
  305.3 4.2 copy-start.8
  318.6 55.8 %copy-start.1 = (f32[32,3456]{0,1:T(8,128)S(1)}, f32[32,3456]{0,1:T(8,128)}, u32[]{:S(2)}) copy-start(f32[32,3456]{0,1:T(8,128)} %copy-done) | copy-start | bytes 1327108
  366.5 8.3 %collective-permute-start.4 = (f32[32,768]{0,1:T(8,128)}, f32[32,768]{0,1:T(8,128)}, u32[]{:S(2)}, u32[]{:S(2)}) collective-permute-start(f32[32,768]{0,1:T(8,128)} %get-tuple-element.6), channel_id=1, source_target_pairs={{1,0},{2,1},{3,2},{4,3},{5,4},{6,5},{7,6},{8,7},{9,8},{10,9},{11,1... | collective-permute-start | bytes 294920 | tf_op jit(solution)/shard_map/ppermute | solution.py:29
  367.8 15.6 %collective-permute-start.5 = (f32[32,768]{0,1:T(8,128)S(1)}, f32[32,768]{0,1:T(8,128)}, u32[]{:S(2)}, u32[]{:S(2)}) collective-permute-start(f32[32,768]{0,1:T(8,128)S(1)} %get-tuple-element.5), channel_id=1, source_target_pairs={{0,1},{1,2},{2,3},{3,4},{4,5},{5,6},{6,7},{7,8},{8,9},{9,10},{10,1... | collective-permute-start | bytes 294920 | tf_op jit(solution)/shard_map/ppermute | solution.py:29
  374.9 1.5 slice-start
  452.1 47.7 %copy-start.3 = (f32[32,3456]{1,0:T(8,128)}, f32[32,3456]{1,0:T(8,128)S(1)}, u32[]{:S(2)}) copy-start(f32[32,3456]{1,0:T(8,128)S(1)} %sub.3) | copy-start | bytes 1327108
where the time goes:
time: 509 us; the launch traced here: 500 us
  other arithmetic  185 us (36%)
  local copies, waits for them, and re-layouts  140 us (28%)
  blocking collectives  132 us (26%)
  matrix products  21.9 us (4%)
  starting transfers between devices  15.8 us (3%)
    scatter-add x2, other arithmetic, spread(): jnp.zeros((tracers, owned + 2 * F), jnp.float32).at[:, slots].add(values)  134 us
    gather x1, local copies, waits for them, and re-layouts, per_device(): gathered = source_values[:, columns].reshape(tracers, pairs, NP)  57.4 us
    psum x1, blocking collectives, per_device(): step_gram = lax.psum(jnp.dot(basis, image.T, precision=high), 'dom')  47.2 us
    psum x1, blocking collectives, per_device(): sums = lax.psum((rhs_gram_local,), 'dom')  45.6 us
    psum x1, blocking collectives, per_device(): gram_new = lax.psum(jnp.dot(residual, residual.T, precision=high), 'dom')  39.1 us
    scatter-add x4, other arithmetic, settle(): return own_part.at[:, highs].add(from_above).at[:, lows].add(from_below)  28.9 us
    gather x1, local copies, waits for them, and re-layouts, per_device(): jnp.concatenate([basis, below, above], axis=1)[:, flat_ids]  27.7 us
    ppermute x6, starting transfers between devices, shifted(): return lax.ppermute(value, axis, pairs)  15.8 us
  transfers between devices with their start and end apart: 6, of which 1 were waited for; matrix products, arithmetic and copies ran while one was open for 4% of the time, Pallas kernels for 0%

commit v1 on v0

v1 whole, which is shorter than its diff:
```python
import functools

import jax
import jax.numpy as jnp
import numpy as np
from jax import lax
from jax.experimental import pallas as pl
from jax.experimental.pallas import tpu as pltpu
from jax.sharding import PartitionSpec as P

TR = 32
NP = 64
NODE_DEV = 3456
F = 768
LO = 384
Q_OWN = NODE_DEV // LO
Q_FACE = F // LO
Q_ALL = Q_OWN + 2 * Q_FACE
OWN = Q_OWN * TR
FACE = Q_FACE * TR
CHUNK = 512
GROUP = 8
MESH = pl.DeviceIdType.MESH
HIGH = lax.Precision.HIGHEST
F32 = jnp.float32
BF16 = jnp.bfloat16
NT = (((1,), (1,)), ((), ()))

line_mass = (
    np.array(
        [
            [128.0, 99.0, -36.0, 19.0],
            [99.0, 648.0, -81.0, -36.0],
            [-36.0, -81.0, 648.0, 99.0],
            [19.0, -36.0, 99.0, 128.0],
        ]
    )
    / 504.0
)
mass_table = np.kron(np.kron(line_mass, line_mass), line_mass)
node_order = np.arange(NP).reshape(NP // 2, 2).T.reshape(-1)
mass_block = np.kron(np.eye(4), mass_table[np.ix_(node_order, node_order)]).astype(np.float32)


def lane_ids(shape):
    return lax.broadcasted_iota(jnp.int32, shape, len(shape) - 1)


def pieces(value):
    first = value.astype(BF16)
    return first, (value - first.astype(F32)).astype(BF16)


def one_hot(lo_row):
    width = lo_row.shape[1]
    rows = lax.broadcasted_iota(jnp.int32, (LO, width), 0)
    return jnp.where(rows == lo_row, 1.0, 0.0).astype(BF16)


def scatter(values, lo_row, q_row, blocks, hot=None):
    hot = one_hot(lo_row) if hot is None else hot
    first, second = pieces(values)
    both = jnp.concatenate([first, second], axis=1)
    q_both = jnp.concatenate([q_row, q_row], axis=1)
    left = jnp.concatenate(
        [both * jnp.where(q_both == q, 1.0, 0.0).astype(BF16) for q in blocks], axis=0
    )
    right = jnp.concatenate([hot, hot], axis=1)
    return lax.dot_general(left, right, NT, preferred_element_type=F32)


def gather(table, lo_row, q_row, blocks, hot=None):
    hot = one_hot(lo_row) if hot is None else hot
    found = jnp.dot(table, jnp.concatenate([hot, hot], axis=0), preferred_element_type=F32)
    total = None
    for at, q in enumerate(blocks):
        part = jnp.where(q_row == q, found[at * TR : (at + 1) * TR], 0.0)
        total = part if total is None else total + part
    return total


def pair_kernel(
    target_ref, source_ref, blocks_ref, values_ref, lo_ref, q_ref, out_ref, flat, table, total
):
    pairs = blocks_ref.shape[0]
    elements = total.shape[0]
    lanes = lane_ids((TR, 128))

    for w in range(elements // 2):
        window = values_ref[:, w * 128 : (w + 1) * 128].astype(F32)
        turned = pltpu.roll(window, 64, 1)
        table[2 * w] = jnp.where(lanes < 64, window, turned).astype(BF16)
        table[2 * w + 1] = jnp.where(lanes < 64, turned, window).astype(BF16)

    def lay_out(g, carry):
        rows = blocks_ref[pl.ds(pl.multiple_of(g * 16, 16), 16), :]
        for c in range(32):
            flat[pl.ds(g * 512 + c, 16, stride=32), :] = rows[:, c * 128 : (c + 1) * 128].astype(F32)
        return carry

    lax.fori_loop(0, pairs // 16, lay_out, 0)
    total[...] = jnp.zeros_like(total)

    def multiply(step, carry):
        left, right = [], []
        for g in range(4):
            p = step * 4 + g
            left.append(table[source_ref[p]])
            block = flat[pl.ds(pl.multiple_of(p * 32, 32), 32), :]
            right.append(jnp.where(lanes < 64, block, 0.0).astype(BF16))
            right.append(jnp.where(lanes < 64, 0.0, block).astype(BF16))
        product = lax.dot_general(
            jnp.concatenate(left, axis=0),
            jnp.concatenate(right, axis=0),
            NT,
            preferred_element_type=F32,
        )
        for g in range(4):
            part = product[g * TR : (g + 1) * TR, (g // 2) * 128 : (g // 2 + 1) * 128]
            keep = (lanes < 64) if g % 2 == 0 else (lanes >= 64)
            at = target_ref[step * 4 + g]
            total[at] = total[at] + jnp.where(keep, part, 0.0)
        return carry

    lax.fori_loop(0, pairs // 4, multiply, 0, unroll=4)
    out_ref[...] = jnp.zeros_like(out_ref)

    def add(step, carry):
        tiles = []
        for m in range(CHUNK // 128):
            even = total[step * (CHUNK // NP) + 2 * m]
            odd = total[step * (CHUNK // NP) + 2 * m + 1]
            tiles.append(
                jnp.where(lanes < 64, even + pltpu.roll(even, 64, 1), odd + pltpu.roll(odd, 64, 1))
            )
        out_ref[...] += scatter(
            jnp.concatenate(tiles, axis=1),
            lo_ref[pl.ds(step, 1), :],
            q_ref[pl.ds(step, 1), :],
            range(Q_ALL),
        )
        return carry

    lax.fori_loop(0, lo_ref.shape[0], add, 0)


def exchange_kernel(
    n,
    ext_ref,
    lo_ref,
    q_ref,
    face_lo_ref,
    face_q_ref,
    scale_ref,
    mass_ref,
    right_ref,
    image_ref,
    gram_ref,
    table,
    ext,
    outgoing,
    incoming,
    near,
    far,
    send_sem,
    recv_sem,
    near_send,
    near_recv,
    far_send,
    far_recv,
):
    me = lax.axis_index("dom")
    group = min(GROUP, n)
    layers = n // group
    spot, layer = lax.rem(me, group), me // group
    has_up, has_down = me < n - 1, me > 0
    near_ids = [layer * group + lax.rem(spot + o, group) for o in range(1, group)]
    far_ids = [lax.rem(layer + o, layers) * group + spot for o in range(1, layers)]
    cross_up = jnp.logical_and(spot == group - 1, has_up)
    cross_down = jnp.logical_and(spot == 0, has_down)

    barrier = pltpu.get_barrier_semaphore()
    for other in near_ids + far_ids:
        pl.semaphore_signal(barrier, inc=1, device_id=(other,), device_id_type=MESH)

    @pl.when(cross_up)
    def _():
        pl.semaphore_signal(barrier, inc=1, device_id=(me + 1,), device_id_type=MESH)

    @pl.when(cross_down)
    def _():
        pl.semaphore_signal(barrier, inc=1, device_id=(me - 1,), device_id_type=MESH)

    partners = group + layers - 2
    crossing = jnp.logical_or(cross_up, cross_down)

    @pl.when(crossing)
    def _():
        pl.semaphore_wait(barrier, partners + 1)

    @pl.when(jnp.logical_not(crossing))
    def _():
        pl.semaphore_wait(barrier, partners)

    def copy(source, phase, way):
        return pltpu.make_async_remote_copy(
            src_ref=source,
            dst_ref=incoming.at[phase, way],
            send_sem=send_sem.at[phase, way],
            recv_sem=recv_sem.at[phase, way],
            device_id=(me + (1 if way else -1),),
            device_id_type=MESH,
        )

    def start(source, phase, way):
        @pl.when(has_up if way else has_down)
        def _():
            copy(source, phase, way).start()

    def finish(source, phase, way):
        @pl.when(has_up if way else has_down)
        def _():
            copy(source, phase, way).wait_send()

    def arrive(source, phase, way):
        @pl.when(has_down if way else has_up)
        def _():
            copy(source, phase, way).wait_recv()

        @pl.when(jnp.logical_not(has_down if way else has_up))
        def _():
            incoming[phase, way] = jnp.zeros((FACE, LO), F32)

    down_rows = pl.ds(OWN, FACE)
    up_rows = pl.ds(OWN + FACE, FACE)
    own_blocks = range(Q_OWN)

    def face_row(ref, at):
        return ref[at : at + 1, :]

    def settle(own, phase):
        for way in range(2):
            for b in range(Q_FACE):
                at = way * Q_FACE + b
                own = own + scatter(
                    incoming[phase, way, b * TR : (b + 1) * TR, :],
                    face_row(face_lo_ref, at),
                    face_row(face_q_ref, at),
                    own_blocks,
                )
        return own

    start(ext_ref.at[down_rows], 0, 0)
    start(ext_ref.at[up_rows], 0, 1)
    arrive(ext_ref.at[down_rows], 0, 0)
    arrive(ext_ref.at[up_rows], 0, 1)
    right = settle(ext_ref[0:OWN, :], 0)
    right_ref[...] = right
    first, second = pieces(right)
    table[0:OWN, 0:LO] = first
    table[0:OWN, LO : 2 * LO] = second

    for way in (1, 0):
        for b in range(Q_FACE):
            at = (1 - way) * Q_FACE + b
            outgoing[way, b * TR : (b + 1) * TR, :] = gather(
                table[0:OWN, :], face_row(face_lo_ref, at), face_row(face_q_ref, at), own_blocks
            )
        start(outgoing.at[way], 1, way)
    for way in (1, 0):
        arrive(outgoing.at[way], 1, way)
        rows = OWN if way else OWN + FACE
        first, second = pieces(incoming[1, way])
        table[rows : rows + FACE, 0:LO] = first
        table[rows : rows + FACE, LO : 2 * LO] = second

    ext[...] = jnp.zeros_like(ext)

    def element_step(step, carry):
        lo_row = lo_ref[pl.ds(step, 1), :]
        q_row = q_ref[pl.ds(step, 1), :]
        hot = one_hot(lo_row)
        found = gather(table[...], lo_row, q_row, range(Q_ALL), hot)
        first, second = pieces(
            jnp.concatenate([found[:, h : h + 256] for h in range(0, CHUNK, 256)], axis=0)
        )
        applied = (
            jnp.dot(first, mass_ref[0], preferred_element_type=F32)
            + jnp.dot(second, mass_ref[0], preferred_element_type=F32)
            + jnp.dot(first, mass_ref[1], preferred_element_type=F32)
        )
        applied = jnp.concatenate(
            [applied[h * TR : (h + 1) * TR] for h in range(CHUNK // 256)], axis=1
        )
        applied = applied * scale_ref[pl.ds(step, 1), :]
        ext[...] += scatter(applied, lo_row, q_row, range(Q_ALL), hot)
        return carry

    lax.fori_loop(0, lo_ref.shape[0], element_step, 0)
    start(ext.at[down_rows], 2, 0)
    start(ext.at[up_rows], 2, 1)
    arrive(ext.at[down_rows], 2, 0)
    arrive(ext.at[up_rows], 2, 1)
    image = settle(ext[0:OWN, :], 2)
    image_ref[...] = image

    nothing = jnp.zeros((TR, LO), F32)
    gram = jnp.zeros((TR, 128), F32)
    for q in range(Q_OWN):
        r = right_ref[q * TR : (q + 1) * TR, :]
        y = image_ref[q * TR : (q + 1) * TR, :]
        gram += lax.dot_general(
            r,
            jnp.concatenate([r, y, nothing, nothing], axis=0),
            NT,
            precision=HIGH,
            preferred_element_type=F32,
        )
        gram += lax.dot_general(
            y,
            jnp.concatenate([nothing, nothing, y, nothing], axis=0),
            NT,
            precision=HIGH,
            preferred_element_type=F32,
        )

    def sum_over(value, buffer, others, sends, recvs):
        buffer[0] = value

        def part(o, other):
            return pltpu.make_async_remote_copy(
                src_ref=buffer.at[0],
                dst_ref=buffer.at[o],
                send_sem=sends.at[o],
                recv_sem=recvs.at[o],
                device_id=(other,),
                device_id_type=MESH,
            )

        for o, other in enumerate(others, 1):
            part(o, other).start()
        for o, other in enumerate(others, 1):
            part(o, other).wait_recv()
            value = value + buffer[o]
        for o, other in enumerate(others, 1):
            part(o, other).wait_send()
        return value

    gram = sum_over(gram, near, near_ids, near_send, near_recv)
    gram_ref[...] = sum_over(gram, far, far_ids, far_send, far_recv)

    finish(ext_ref.at[down_rows], 0, 0)
    finish(ext_ref.at[up_rows], 0, 1)
    for way in range(2):
        finish(outgoing.at[way], 1, way)
    finish(ext.at[down_rows], 2, 0)
    finish(ext.at[up_rows], 2, 1)


def output_kernel(gram_ref, right_ref, image_ref, solution_ref, residual_ref, basis_ref):
    def dot(a, b):
        return jnp.dot(a, b, precision=HIGH, preferred_element_type=F32)

    rows = lax.broadcasted_iota(jnp.int32, (TR, 128), 0)
    lanes = lane_ids((TR, 128))
    work = gram_ref[...]
    gram = work[:, 0:TR]
    for j in range(TR):
        pivot = work[j : j + 1, :] / work[j : j + 1, TR + j : TR + j + 1]
        work = jnp.where(rows == j, pivot, work - work[:, TR + j : TR + j + 1] * pivot)
    step_t = work[:, 0:TR]
    step = step_t.T
    image_part = work[:, 2 * TR : 3 * TR]
    new_gram = dot(gram, dot(image_part, step_t)) - gram
    work = jnp.concatenate([new_gram, jnp.zeros((TR, 128 - TR), F32)], axis=1)
    work = jnp.where(lanes == rows + TR, 1.0, work)
    scale = jnp.zeros((TR, 128), F32)
    for j in range(TR):
        pivot = work[j : j + 1, j : j + 1]
        scale = jnp.where(rows == j, lax.rsqrt(pivot), scale)
        factor = work[:, j : j + 1] / pivot
        work = jnp.where(rows > j, work - factor * work[j : j + 1, :], work)
    lower = (work * scale)[:, TR : 2 * TR]
    for q in range(Q_OWN):
        at = slice(q * LO, (q + 1) * LO)
        r = right_ref[q * TR : (q + 1) * TR, :]
        left = r - dot(step, image_ref[q * TR : (q + 1) * TR, :])
        solution_ref[:, at] = dot(step, r)
        residual_ref[:, at] = left
        basis_ref[:, at] = dot(lower, left)


def per_device(
    n, connectivity, send_down, send_up, jacobian, pair_blocks, pair_target, pair_source, source_values
):
    elements = connectivity.shape[0]
    pairs = pair_target.shape[0]
    chunks = elements * NP // CHUNK
    vmem = pl.BlockSpec(memory_space=pltpu.VMEM)
    smem = pl.BlockSpec(memory_space=pltpu.SMEM)

    slots = connectivity.reshape(elements, NP // 2, 2).transpose(0, 2, 1).reshape(chunks, CHUNK)
    q_ids = slots // LO
    lo_ids = slots - q_ids * LO
    faces = jnp.concatenate([send_up[0].reshape(Q_FACE, LO), send_down[0].reshape(Q_FACE, LO)])
    face_q = faces // LO
    face_lo = faces - face_q * LO
    scale = jnp.repeat(jacobian, NP).reshape(chunks, CHUNK)
    mass = jnp.asarray(mass_block)
    mass_first = mass.astype(BF16)
    mass_pair = jnp.stack([mass_first, (mass - mass_first.astype(F32)).astype(BF16)])

    ext = pl.pallas_call(
        pair_kernel,
        out_shape=jax.ShapeDtypeStruct((Q_ALL * TR, LO), F32),
        in_specs=[smem, smem, vmem, vmem, vmem, vmem],
        out_specs=vmem,
        scratch_shapes=[
            pltpu.VMEM((pairs * 32, 128), F32),
            pltpu.VMEM((elements, TR, 128), BF16),
            pltpu.VMEM((elements, TR, 128), F32),
        ],
        compiler_params=pltpu.CompilerParams(vmem_limit_bytes=48 * 2**20),
        name="pair_stage",
    )(pair_target, pair_source, pair_blocks, source_values, lo_ids, q_ids)

    group = min(GROUP, n)
    layers = n // group
    field = jax.ShapeDtypeStruct((OWN, LO), F32)
    right, image, gram = pl.pallas_call(
        functools.partial(exchange_kernel, n),
        out_shape=(field, field, jax.ShapeDtypeStruct((TR, 128), F32)),
        in_specs=[vmem] * 7,
        out_specs=(vmem, vmem, vmem),
        scratch_shapes=[
            pltpu.VMEM((Q_ALL * TR, 2 * LO), BF16),
            pltpu.VMEM((Q_ALL * TR, LO), F32),
            pltpu.VMEM((2, FACE, LO), F32),
            pltpu.VMEM((3, 2, FACE, LO), F32),
            pltpu.VMEM((group, TR, 128), F32),
            pltpu.VMEM((layers, TR, 128), F32),
            pltpu.SemaphoreType.DMA((3, 2)),
            pltpu.SemaphoreType.DMA((3, 2)),
            pltpu.SemaphoreType.DMA((group,)),
            pltpu.SemaphoreType.DMA((group,)),
            pltpu.SemaphoreType.DMA((layers,)),
            pltpu.SemaphoreType.DMA((layers,)),
        ],
        compiler_params=pltpu.CompilerParams(
            collective_id=0, has_side_effects=True, vmem_limit_bytes=48 * 2**20
        ),
        name="exchange_stage",
    )(ext, lo_ids, q_ids, face_lo, face_q, scale, mass_pair)

    out = jax.ShapeDtypeStruct((TR, NODE_DEV), F32)
    return pl.pallas_call(
        output_kernel,
        out_shape=(out, out, out),
        in_specs=[vmem] * 3,
        out_specs=(vmem, vmem, vmem),
        compiler_params=pltpu.CompilerParams(vmem_limit_bytes=32 * 2**20),
        name="output_stage",
    )(gram, right, image)


def solution(mesh):
    return jax.shard_map(
        functools.partial(per_device, mesh.shape["dom"]),
        mesh=mesh,
        in_specs=(
            P("dom", None),
            P("dom", None),
            P("dom", None),
            P("dom"),
            P("dom", None),
            P("dom"),
            P("dom"),
            P(None, "dom"),
        ),
        out_specs=(P(None, "dom"), P(None, "dom"), P(None, "dom")),
        check_vma=False,
    )
```

time: 509 us -> 88.1 us (0.17); the launches traced: 500 us -> 87.7 us
  other arithmetic: 185 us -> 1.49 us
  local copies, waits for them, and re-layouts: 140 us -> 5.98 us
  blocking collectives: 132 us -> 0 us
  Pallas kernels: 0 us -> 79.6 us
  matrix products: 21.9 us -> 0 us
  starting transfers between devices: 15.8 us -> 0 us
    scatter-add x6 -> x0, other arithmetic: 163 us -> none  [the longest x2 134 us: spread(): jnp.zeros((tracers, owned + 2 * F), jnp.float32).at[:, slots].add(values)]
    psum x3 -> x0, blocking collectives: 132 us -> none  [the longest x1 47.2 us: per_device(): step_gram = lax.psum(jnp.dot(basis, image.T, precision=high), 'dom')]
    gather x7 -> x0, local copies, waits for them, and re-layouts: 92.1 us -> none  [the longest x1 57.4 us: per_device(): gathered = source_values[:, columns].reshape(tracers, pairs, NP)]
    pallas_call x0 -> x3, Pallas kernels: none -> 79.6 us  [the longest x1 51.4 us: per_device(): pl.pallas_call(functools.partial(exchange_kernel, n), out_shape=(field, f...]
    reshape x8 -> x2, local copies, waits for them, and re-layouts: 24.6 us -> 1.07 us  [per_device(): connectivity.reshape(elements, NP // 2, 2).transpose(0, 2, 1)]
    another operation x15 -> x0, other arithmetic: 20 us -> none  [the longest x4 6.17 us: lower_solve(): return jax.scipy.linalg.solve_triangular(lower, matrix, lower=True)]
    dot_general x7 -> x0, matrix products: 17.5 us -> none  [the longest x1 5.79 us: per_device(): jnp.einsum('pij,tpj->tpi', mixed, gathered, preferred_element_type=jnp.fl...]
    ppermute x6 -> x0, starting transfers between devices: 15.8 us -> none  [shifted(): return lax.ppermute(value, axis, pairs)]
  transfers between devices with their start and end apart: 6 -> 0, of which waited for: 1 -> 0; matrix products, arithmetic and copies ran while one was open for 4% -> 0% of each run, Pallas kernels for 0% -> 0%
where the time goes in v1:
time: 88.1 us; the launch traced here: 87.7 us
  Pallas kernels  79.6 us (90%)
  local copies, waits for them, and re-layouts  5.98 us (7%)
  other arithmetic  1.49 us (2%)
    pallas_call x1, Pallas kernels, per_device(): pl.pallas_call(functools.partial(exchange_kernel, n), out_shape=(field, f...  51.4 us
    pallas_call x1, Pallas kernels, per_device(): pl.pallas_call(pair_kernel, out_shape=jax.ShapeDtypeStruct((Q_ALL * TR, L...  19.6 us
    pallas_call x1, Pallas kernels, per_device(): pl.pallas_call(output_kernel, out_shape=(out, out, out), in_specs=[vmem]...  8.55 us
    unnamed x10, local copies, waits for them, and re-layouts  3.99 us

profile of v1, /device:TPU:0, one launch (start us, length us, event | category | flops | bytes accessed | tf_op | source)
XLA Modules:
  0.0 87.7 jit_solution(1906073237286398024)
XLA Ops:
  0.6 0.0 copy-start.2
  0.6 0.7 reduce.1
  1.4 0.7 reduce
  2.1 0.7 broadcast_in_dim.7
  2.9 0.1 broadcast_in_dim.8
  3.0 0.1 broadcast_in_dim.9.scale_ref
  3.0 0.9 copy.13
  3.9 0.2 reshape.15
  4.1 0.0 copy-start
  4.2 1.6 %copy-done = bf16[256,4096]{1,0:T(8,128)(2,1)S(1)} copy-done((bf16[256,4096]{1,0:T(8,128)(2,1)S(1)}, bf16[256,4096]{1,0:T(8,128)(2,1)}, u32[]{:S(2)}) %copy-start) | copy-done | bytes 2097176
  5.7 0.0 copy-start.1
  5.7 1.0 %copy-done.1 = bf16[32,8192]{1,0:T(8,128)(2,1)S(1)} copy-done((bf16[32,8192]{1,0:T(8,128)(2,1)S(1)}, bf16[32,8192]{1,0:T(8,128)(2,1)}, u32[]{:S(2)}) %copy-start.1) | copy-done | bytes 524312
  6.8 0.0 copy-start.3
  6.8 0.7 copy-done.3
  7.5 0.0 copy-start.4
  7.5 0.7 copy-done.4
  8.1 19.6 %pair_stage.1.ext_ref = f32[416,384]{1,0:T(8,128)S(1)} custom-call(s32[256]{0:T(256)S(1)} %copy-done.3, s32[256]{0:T(256)S(1)} %copy-done.4, bf16[256,4096]{1,0:T(8,128)(2,1)S(1)} %copy-done, bf16[32,8192]{1,0:T(8,128)(2,1)S(1)} %copy-done.1, s32[16,512]{1,0:T(8,128)S(1)} %get-tuple-element.12.lo_ref, s32[16,512]{1,0:T(8,128)S(1)} %get-tuple-element.11.q_ref), custom_call_target="tpu_custom_call" | custom-call | tf_op jit(solution)/shard_map/pair_stage/pallas_call | solution.py:413
  27.7 0.0 copy-done.2
  27.8 51.4 %exchange_stage.1 = (f32[288,384]{1,0:T(8,128)S(1)}, f32[288,384]{1,0:T(8,128)S(1)}, f32[32,128]{1,0:T(8,128)S(1)}) custom-call(f32[416,384]{1,0:T(8,128)S(1)} %pair_stage.1.ext_ref, s32[16,512]{1,0:T(8,128)S(1)} %get-tuple-element.12.lo_ref, s32[16,512]{1,0:T(8,128)S(1)} %get-tuple-element.11.q_ref, s32[4,384]{1,0:T(4,128)S(1)} %get-tuple-element.9.face_lo_ref, ...), custom_call_target="tpu_custom_call" | custom-call | tf_op jit(solution)/shard_map/exchange_stage/pallas_call | solution.py:430
  79.2 8.6 %output_stage.1 = (f32[32,3456]{1,0:T(8,128)}, f32[32,3456]{1,0:T(8,128)}, f32[32,3456]{1,0:T(8,128)}) custom-call(f32[32,128]{1,0:T(8,128)S(1)} %get-tuple-element.6.gram_ref, f32[288,384]{1,0:T(8,128)S(1)} %get-tuple-element.7.right_ref, f32[288,384]{1,0:T(8,128)S(1)} %get-tuple-element.8.image_ref), custom_call_target="tpu_custom_call" | custom-call | tf_op jit(solution)/shard_map/output_stage/pallas_call | solution.py:456
  (4 shorter events, 0.1 us)
Async XLA Ops:
  0.6 27.1 %copy-start.2 = (bf16[2,256,256]{2,1,0:T(8,128)(2,1)S(1)}, bf16[2,256,256]{2,1,0:T(8,128)(2,1)}, u32[]{:S(2)}) copy-start(bf16[2,256,256]{2,1,0:T(8,128)(2,1)} %constant.29.mass_ref) | copy-start | bytes 786436
  4.1 1.6 %copy-start = (bf16[256,4096]{1,0:T(8,128)(2,1)S(1)}, bf16[256,4096]{1,0:T(8,128)(2,1)}, u32[]{:S(2)}) copy-start(bf16[256,4096]{1,0:T(8,128)(2,1)} %blocks_ref.1) | copy-start | bytes 6291460
  5.7 1.0 %copy-start.1 = (bf16[32,8192]{1,0:T(8,128)(2,1)S(1)}, bf16[32,8192]{1,0:T(8,128)(2,1)}, u32[]{:S(2)}) copy-start(bf16[32,8192]{1,0:T(8,128)(2,1)} %values_ref.1) | copy-start | bytes 1572868
  6.8 0.7 copy-start.3
  7.5 0.7 copy-start.4

commit v2 on v1

--- a/solution.py
+++ b/solution.py
@@ -2,6 +2,7 @@
 
 import jax
 import jax.numpy as jnp
+import ml_dtypes
 import numpy as np
 from jax import lax
 from jax.experimental import pallas as pl
@@ -40,6 +41,11 @@
 mass_table = np.kron(np.kron(line_mass, line_mass), line_mass)
 node_order = np.arange(NP).reshape(NP // 2, 2).T.reshape(-1)
 mass_block = np.kron(np.eye(4), mass_table[np.ix_(node_order, node_order)]).astype(np.float32)
+mass_first = mass_block.astype(ml_dtypes.bfloat16)
+mass_pair = np.stack(
+    [mass_first, (mass_block - mass_first.astype(np.float32)).astype(ml_dtypes.bfloat16)]
+)
+order_table = np.tile(np.eye(NP, dtype=np.float32)[:, node_order], (1, 2))
 
 
 def lane_ids(shape):
@@ -57,21 +63,22 @@
     return jnp.where(rows == lo_row, 1.0, 0.0).astype(BF16)
 
 
-def scatter(values, lo_row, q_row, blocks, hot=None):
-    hot = one_hot(lo_row) if hot is None else hot
-    first, second = pieces(values)
-    both = jnp.concatenate([first, second], axis=1)
-    q_both = jnp.concatenate([q_row, q_row], axis=1)
-    left = jnp.concatenate(
+def spread(both, q_both, blocks):
+    return jnp.concatenate(
         [both * jnp.where(q_both == q, 1.0, 0.0).astype(BF16) for q in blocks], axis=0
     )
-    right = jnp.concatenate([hot, hot], axis=1)
+
+
+def twice(value, axis):
+    return jnp.concatenate([value, value], axis=axis)
+
+
+def add_up(left, right):
     return lax.dot_general(left, right, NT, preferred_element_type=F32)
 
 
-def gather(table, lo_row, q_row, blocks, hot=None):
-    hot = one_hot(lo_row) if hot is None else hot
-    found = jnp.dot(table, jnp.concatenate([hot, hot], axis=0), preferred_element_type=F32)
+def gather(table, q_row, blocks, hot):
+    found = jnp.dot(table, twice(hot, 0), preferred_element_type=F32)
     total = None
     for at, q in enumerate(blocks):
         part = jnp.where(q_row == q, found[at * TR : (at + 1) * TR], 0.0)
@@ -79,18 +86,76 @@
     return total
 
 
+def split_slots(slots):
+    q = jnp.right_shift(jnp.right_shift(slots, 7) * 43, 7)
+    return q, slots - q * LO
+
+
 def pair_kernel(
-    target_ref, source_ref, blocks_ref, values_ref, lo_ref, q_ref, out_ref, flat, table, total
+    target_ref,
+    source_ref,
+    blocks_hbm,
+    values_ref,
+    slots_ref,
+    jacobian_ref,
+    order_ref,
+    out_ref,
+    lo_ref,
+    q_ref,
+    scale_ref,
+    blocks_ref,
+    flat,
+    table,
+    total,
+    wide,
+    blocks_sem,
 ):
     pairs = blocks_ref.shape[0]
     elements = total.shape[0]
+    chunks = lo_ref.shape[0]
+    per_chunk = CHUNK // NP
     lanes = lane_ids((TR, 128))
+
+    fetch = pltpu.make_async_copy(blocks_hbm, blocks_ref, blocks_sem)
+    fetch.start()
+
+    def by_chunk():
+        left_half = lane_ids((chunks, 128)) < 64
+        return jnp.concatenate(
+            [
+                jnp.where(
+                    left_half,
+                    wide[pl.ds(2 * m, chunks, stride=per_chunk), :],
+                    wide[pl.ds(2 * m + 1, chunks, stride=per_chunk), :],
+                )
+                for m in range(CHUNK // 128)
+            ],
+            axis=1,
+        )
+
+    wide[...] = jnp.dot(
+        slots_ref[...].astype(F32), order_ref[...], precision=HIGH, preferred_element_type=F32
+    )
+    q_ids, lo_ids = split_slots((by_chunk() + 0.5).astype(jnp.int32))
+    q_ref[...] = q_ids
+    lo_ref[...] = lo_ids
+    corner = lax.broadcasted_iota(jnp.int32, (elements, elements), 0) == lane_ids((elements, elements))
+    wide[...] = jnp.dot(
+        jnp.where(corner, jacobian_ref[...], 0.0),
+        jnp.ones((elements, 128), F32),
+        precision=HIGH,
+        preferred_element_type=F32,
+    )
+    scale_ref[...] = by_chunk()
 
     for w in range(elements // 2):
         window = values_ref[:, w * 128 : (w + 1) * 128].astype(F32)
         turned = pltpu.roll(window, 64, 1)
         table[2 * w] = jnp.where(lanes < 64, window, turned).astype(BF16)
         table[2 * w + 1] = jnp.where(lanes < 64, turned, window).astype(BF16)
+    total[...] = jnp.zeros_like(total)
+    out_ref[...] = jnp.zeros_like(out_ref)
+    fetch.wait()
 
     def lay_out(g, carry):
         rows = blocks_ref[pl.ds(pl.multiple_of(g * 16, 16), 16), :]
@@ -99,7 +164,6 @@
         return carry
 
     lax.fori_loop(0, pairs // 16, lay_out, 0)
-    total[...] = jnp.zeros_like(total)
 
     def multiply(step, carry):
         left, right = [], []
@@ -109,12 +173,7 @@
             block = flat[pl.ds(pl.multiple_of(p * 32, 32), 32), :]
             right.append(jnp.where(lanes < 64, block, 0.0).astype(BF16))
             right.append(jnp.where(lanes < 64, 0.0, block).astype(BF16))
-        product = lax.dot_general(
-            jnp.concatenate(left, axis=0),
-            jnp.concatenate(right, axis=0),
-            NT,
-            preferred_element_type=F32,
-        )
+        product = add_up(jnp.concatenate(left, axis=0), jnp.concatenate(right, axis=0))
         for g in range(4):
             part = product[g * TR : (g + 1) * TR, (g // 2) * 128 : (g // 2 + 1) * 128]
             keep = (lanes < 64) if g % 2 == 0 else (lanes >= 64)
@@ -122,26 +181,23 @@
             total[at] = total[at] + jnp.where(keep, part, 0.0)
         return carry
 
-    lax.fori_loop(0, pairs // 4, multiply, 0, unroll=4)
-    out_ref[...] = jnp.zeros_like(out_ref)
+    lax.fori_loop(0, pairs // 4, multiply, 0, unroll=8)
 
     def add(step, carry):
         tiles = []
         for m in range(CHUNK // 128):
-            even = total[step * (CHUNK // NP) + 2 * m]
-            odd = total[step * (CHUNK // NP) + 2 * m + 1]
+            even = total[step * per_chunk + 2 * m]
+            odd = total[step * per_chunk + 2 * m + 1]
             tiles.append(
                 jnp.where(lanes < 64, even + pltpu.roll(even, 64, 1), odd + pltpu.roll(odd, 64, 1))
             )
-        out_ref[...] += scatter(
-            jnp.concatenate(tiles, axis=1),
-            lo_ref[pl.ds(step, 1), :],
-            q_ref[pl.ds(step, 1), :],
-            range(Q_ALL),
-        )
+        both = jnp.concatenate(pieces(jnp.concatenate(tiles, axis=1)), axis=1)
+        q_both = twice(q_ref[pl.ds(step, 1), :], 1)
+        hot = one_hot(lo_ref[pl.ds(step, 1), :])
+        out_ref[...] += add_up(spread(both, q_both, range(Q_ALL)), twice(hot, 1))
         return carry
 
-    lax.fori_loop(0, lo_ref.shape[0], add, 0)
+    lax.fori_loop(0, chunks, add, 0, unroll=2)
 
 
 def exchange_kernel(
@@ -149,14 +205,18 @@
     ext_ref,
     lo_ref,
     q_ref,
-    face_lo_ref,
-    face_q_ref,
     scale_ref,
+    up_ref,
+    down_ref,
     mass_ref,
     right_ref,
     image_ref,
     gram_ref,
     table,
+    hot,
+    face_hot,
+    found,
+    applied,
     ext,
     outgoing,
     incoming,
@@ -233,40 +293,55 @@
 
     down_rows = pl.ds(OWN, FACE)
     up_rows = pl.ds(OWN + FACE, FACE)
-    own_blocks = range(Q_OWN)
-
-    def face_row(ref, at):
-        return ref[at : at + 1, :]
+    own_blocks, face_blocks = range(Q_OWN), range(Q_OWN, Q_ALL)
+    chunks = lo_ref.shape[0]
+
+    start(ext_ref.at[down_rows], 0, 0)
+    start(ext_ref.at[up_rows], 0, 1)
+
+    def mark(step, carry):
+        hot[step] = one_hot(lo_ref[pl.ds(step, 1), :])
+        return carry
+
+    lax.fori_loop(0, chunks, mark, 0)
+    faces = [split_slots(up_ref[...]), split_slots(down_ref[...])]
+    for way in range(2):
+        face_hot[way] = one_hot(faces[way][1])
 
     def settle(own, phase):
+        left, right = [], []
         for way in range(2):
             for b in range(Q_FACE):
-                at = way * Q_FACE + b
-                own = own + scatter(
-                    incoming[phase, way, b * TR : (b + 1) * TR, :],
-                    face_row(face_lo_ref, at),
-                    face_row(face_q_ref, at),
-                    own_blocks,
+                part = slice(b * LO, (b + 1) * LO)
+                both = jnp.concatenate(
+                    pieces(incoming[phase, way, b * TR : (b + 1) * TR, :]), axis=1
                 )
-        return own
-
-    start(ext_ref.at[down_rows], 0, 0)
-    start(ext_ref.at[up_rows], 0, 1)
+                left.append(spread(both, twice(faces[way][0][:, part], 1), own_blocks))
+                right.append(twice(face_hot[way, :, part], 1))
+        return own + add_up(jnp.concatenate(left, axis=1), jnp.concatenate(right, axis=1))
+
     arrive(ext_ref.at[down_rows], 0, 0)
     arrive(ext_ref.at[up_rows], 0, 1)
     right = settle(ext_ref[0:OWN, :], 0)
-    right_ref[...] = right
     first, second = pieces(right)
     table[0:OWN, 0:LO] = first
     table[0:OWN, LO : 2 * LO] = second
 
     for way in (1, 0):
+        values = gather(table[0:OWN, :], faces[1 - way][0], own_blocks, face_hot[1 - way])
         for b in range(Q_FACE):
-            at = (1 - way) * Q_FACE + b
-            outgoing[way, b * TR : (b + 1) * TR, :] = gather(
-                table[0:OWN, :], face_row(face_lo_ref, at), face_row(face_q_ref, at), own_blocks
-            )
+            outgoing[way, b * TR : (b + 1) * TR, :] = values[:, b * LO : (b + 1) * LO]
         start(outgoing.at[way], 1, way)
+
+    def own_values(step, carry):
+        q_row = q_ref[pl.ds(step, 1), :]
+        found[step] = gather(table[0:OWN, :], q_row, own_blocks, hot[step])
+        return carry
+
+    lax.fori_loop(0, chunks, own_values, 0, unroll=2)
+    for q in own_blocks:
+        right_ref[:, q * LO : (q + 1) * LO] = right[q * TR : (q + 1) * TR]
+    ext[...] = jnp.zeros_like(ext)
     for way in (1, 0):
         arrive(outgoing.at[way], 1, way)
         rows = OWN if way else OWN + FACE
@@ -274,55 +349,61 @@
         table[rows : rows + FACE, 0:LO] = first
         table[rows : rows + FACE, LO : 2 * LO] = second
 
-    ext[...] = jnp.zeros_like(ext)
-
-    def element_step(step, carry):
-        lo_row = lo_ref[pl.ds(step, 1), :]
+    def elements(step, carry):
         q_row = q_ref[pl.ds(step, 1), :]
-        hot = one_hot(lo_row)
-        found = gather(table[...], lo_row, q_row, range(Q_ALL), hot)
+        values = found[step] + gather(table[OWN:, :], q_row, face_blocks, hot[step])
         first, second = pieces(
-            jnp.concatenate([found[:, h : h + 256] for h in range(0, CHUNK, 256)], axis=0)
+            jnp.concatenate([values[:, h : h + 256] for h in range(0, CHUNK, 256)], axis=0)
         )
-        applied = (
+        result = (
             jnp.dot(first, mass_ref[0], preferred_element_type=F32)
             + jnp.dot(second, mass_ref[0], preferred_element_type=F32)
             + jnp.dot(first, mass_ref[1], preferred_element_type=F32)
         )
-        applied = jnp.concatenate(
-            [applied[h * TR : (h + 1) * TR] for h in range(CHUNK // 256)], axis=1
+        result = jnp.concatenate(
+            [result[h * TR : (h + 1) * TR] for h in range(CHUNK // 256)], axis=1
         )
-        applied = applied * scale_ref[pl.ds(step, 1), :]
-        ext[...] += scatter(applied, lo_row, q_row, range(Q_ALL), hot)
+        both = jnp.concatenate(pieces(result * scale_ref[pl.ds(step, 1), :]), axis=1)
+        applied[step] = both
+        ext[OWN:, :] += add_up(spread(both, twice(q_row, 1), face_blocks), twice(hot[step], 1))
         return carry
 
-    lax.fori_loop(0, lo_ref.shape[0], element_step, 0)
+    lax.fori_loop(0, chunks, elements, 0, unroll=2)
     start(ext.at[down_rows], 2, 0)
     start(ext.at[up_rows], 2, 1)
+
+    def own_sums(step, carry):
+        q_both = twice(q_ref[pl.ds(step, 1), :], 1)
+        ext[0:OWN, :] += add_up(spread(applied[step], q_both, own_blocks), twice(hot[step], 1))
+        return carry
+
+    lax.fori_loop(0, chunks, own_sums, 0, unroll=2)
     arrive(ext.at[down_rows], 2, 0)
     arrive(ext.at[up_rows], 2, 1)
     image = settle(ext[0:OWN, :], 2)
-    image_ref[...] = image
-
-    nothing = jnp.zeros((TR, LO), F32)
-    gram = jnp.zeros((TR, 128), F32)
-    for q in range(Q_OWN):
-        r = right_ref[q * TR : (q + 1) * TR, :]
-        y = image_ref[q * TR : (q + 1) * TR, :]
-        gram += lax.dot_general(
-            r,
-            jnp.concatenate([r, y, nothing, nothing], axis=0),
-            NT,
-            precision=HIGH,
-            preferred_element_type=F32,
-        )
-        gram += lax.dot_general(
-            y,
-            jnp.concatenate([nothing, nothing, y, nothing], axis=0),
-            NT,
-            precision=HIGH,
-            preferred_element_type=F32,
-        )
+    for q in own_blocks:
+        image_ref[:, q * LO : (q + 1) * LO] = image[q * TR : (q + 1) * TR]
+
+    def as_row(value):
+        return jnp.concatenate([value[q * TR : (q + 1) * TR] for q in own_blocks], axis=1)
+
+    first, second = pieces(image)
+    stack = jnp.concatenate(
+        [
+            as_row(table[0:OWN, 0:LO]),
+            as_row(table[0:OWN, LO : 2 * LO]),
+            as_row(first),
+            as_row(second),
+        ],
+        axis=0,
+    )
+    products = add_up(stack, stack)
+    lanes = lane_ids((TR, 128))
+    upper = products[0:TR] + products[TR : 2 * TR]
+    lower = products[2 * TR : 3 * TR] + products[3 * TR :]
+    upper = upper + pltpu.roll(upper, 96, 1)
+    lower = pltpu.roll(lower + pltpu.roll(lower, 96, 1), 96, 1)
+    gram = jnp.where(jnp.logical_and(lanes >= TR, lanes < 2 * TR), lower, upper)
 
     def sum_over(value, buffer, others, sends, recvs):
         buffer[0] = value
@@ -365,29 +446,59 @@
     lanes = lane_ids((TR, 128))
     work = gram_ref[...]
     gram = work[:, 0:TR]
-    for j in range(TR):
-        pivot = work[j : j + 1, :] / work[j : j + 1, TR + j : TR + j + 1]
-        work = jnp.where(rows == j, pivot, work - work[:, TR + j : TR + j + 1] * pivot)
+    for j in range(0, TR, 2):
+        c = 2 * TR + j
+        a, b = work[j : j + 1, :], work[j + 1 : j + 2, :]
+        inverse = 1.0 / a[:, c : c + 1]
+        across = a[:, c + 1 : c + 2] * inverse
+        b = b - (b[:, c : c + 1] * inverse) * a
+        b = b * (1.0 / b[:, c + 1 : c + 2])
+        a = a * inverse - across * b
+        rest = work - work[:, c : c + 1] * a - work[:, c + 1 : c + 2] * b
+        work = jnp.where(rows == j, a, jnp.where(rows == j + 1, b, rest))
     step_t = work[:, 0:TR]
     step = step_t.T
-    image_part = work[:, 2 * TR : 3 * TR]
+    image_part = work[:, TR : 2 * TR]
     new_gram = dot(gram, dot(image_part, step_t)) - gram
+
+    def times(small):
+        first, second = pieces(small)
+        both = jnp.concatenate([first, second], axis=0)
+
+        def apply(value):
+            top, rest = pieces(value)
+            found = jnp.dot(both, top, preferred_element_type=F32)
+            return (
+                found[0:TR] + found[TR : 2 * TR] + jnp.dot(first, rest, preferred_element_type=F32)
+            )
+
+        return apply
+
+    parts = [slice(at, at + 3 * LO) for at in range(0, Q_OWN * LO, 3 * LO)]
+    apply_step = times(step)
+    for part in parts:
+        right = right_ref[:, part]
+        solution_ref[:, part] = apply_step(right)
+        residual_ref[:, part] = right - apply_step(image_ref[:, part])
+
     work = jnp.concatenate([new_gram, jnp.zeros((TR, 128 - TR), F32)], axis=1)
     work = jnp.where(lanes == rows + TR, 1.0, work)
     scale = jnp.zeros((TR, 128), F32)
-    for j in range(TR):
-        pivot = work[j : j + 1, j : j + 1]
+    for j in range(0, TR, 2):
+        a, b = work[j : j + 1, :], work[j + 1 : j + 2, :]
+        pivot, across = a[:, j : j + 1], a[:, j + 1 : j + 2]
+        inverse = 1.0 / pivot
+        b = b - (b[:, j : j + 1] * inverse) * a
+        second_pivot = b[:, j + 1 : j + 2]
+        factor = work[:, j : j + 1] * inverse
+        second = (work[:, j + 1 : j + 2] - factor * across) * (1.0 / second_pivot)
+        rest = work - factor * a - second * b
+        work = jnp.where(rows > j + 1, rest, jnp.where(rows == j + 1, b, work))
         scale = jnp.where(rows == j, lax.rsqrt(pivot), scale)
-        factor = work[:, j : j + 1] / pivot
-        work = jnp.where(rows > j, work - factor * work[j : j + 1, :], work)
-    lower = (work * scale)[:, TR : 2 * TR]
-    for q in range(Q_OWN):
-        at = slice(q * LO, (q + 1) * LO)
-        r = right_ref[q * TR : (q + 1) * TR, :]
-        left = r - dot(step, image_ref[q * TR : (q + 1) * TR, :])
-        solution_ref[:, at] = dot(step, r)
-        residual_ref[:, at] = left
-        basis_ref[:, at] = dot(lower, left)
+        scale = jnp.where(rows == j + 1, lax.rsqrt(second_pivot), scale)
+    apply_lower = times((work * scale)[:, TR : 2 * TR])
+    for part in parts:
+        basis_ref[:, part] = apply_lower(residual_ref[:, part])
 
 
 def per_device(
@@ -399,34 +510,40 @@
     vmem = pl.BlockSpec(memory_space=pltpu.VMEM)
     smem = pl.BlockSpec(memory_space=pltpu.SMEM)
 
-    slots = connectivity.reshape(elements, NP // 2, 2).transpose(0, 2, 1).reshape(chunks, CHUNK)
-    q_ids = slots // LO
-    lo_ids = slots - q_ids * LO
-    faces = jnp.concatenate([send_up[0].reshape(Q_FACE, LO), send_down[0].reshape(Q_FACE, LO)])
-    face_q = faces // LO
-    face_lo = faces - face_q * LO
-    scale = jnp.repeat(jacobian, NP).reshape(chunks, CHUNK)
-    mass = jnp.asarray(mass_block)
-    mass_first = mass.astype(BF16)
-    mass_pair = jnp.stack([mass_first, (mass - mass_first.astype(F32)).astype(BF16)])
-
-    ext = pl.pallas_call(
+    ids = jax.ShapeDtypeStruct((chunks, CHUNK), jnp.int32)
+    ext, lo_ids, q_ids, scale = pl.pallas_call(
         pair_kernel,
-        out_shape=jax.ShapeDtypeStruct((Q_ALL * TR, LO), F32),
-        in_specs=[smem, smem, vmem, vmem, vmem, vmem],
-        out_specs=vmem,
+        out_shape=(
+            jax.ShapeDtypeStruct((Q_ALL * TR, LO), F32),
+            ids,
+            ids,
+            jax.ShapeDtypeStruct((chunks, CHUNK), F32),
+        ),
+        in_specs=[smem, smem, pl.BlockSpec(memory_space=pl.ANY), vmem, vmem, vmem, vmem],
+        out_specs=(vmem,) * 4,
         scratch_shapes=[
+            pltpu.VMEM(pair_blocks.shape, BF16),
             pltpu.VMEM((pairs * 32, 128), F32),
             pltpu.VMEM((elements, TR, 128), BF16),
             pltpu.VMEM((elements, TR, 128), F32),
+            pltpu.VMEM((elements, 128), F32),
+            pltpu.SemaphoreType.DMA,
         ],
         compiler_params=pltpu.CompilerParams(vmem_limit_bytes=48 * 2**20),
         name="pair_stage",
-    )(pair_target, pair_source, pair_blocks, source_values, lo_ids, q_ids)
+    )(
+        pair_target,
+        pair_source,
+        pair_blocks,
+        source_values,
+        connectivity,
+        jacobian.reshape(1, elements),
+        jnp.asarray(order_table),
+    )
 
     group = min(GROUP, n)
     layers = n // group
-    field = jax.ShapeDtypeStruct((OWN, LO), F32)
+    field = jax.ShapeDtypeStruct((TR, NODE_DEV), F32)
     right, image, gram = pl.pallas_call(
         functools.partial(exchange_kernel, n),
         out_shape=(field, field, jax.ShapeDtypeStruct((TR, 128), F32)),
@@ -434,6 +551,10 @@
         out_specs=(vmem, vmem, vmem),
         scratch_shapes=[
             pltpu.VMEM((Q_ALL * TR, 2 * LO), BF16),
+            pltpu.VMEM((chunks, LO, CHUNK), BF16),
+            pltpu.VMEM((2, LO, F), BF16),
+            pltpu.VMEM((chunks, TR, CHUNK), F32),
+            pltpu.VMEM((chunks, TR, 2 * CHUNK), BF16),
             pltpu.VMEM((Q_ALL * TR, LO), F32),
             pltpu.VMEM((2, FACE, LO), F32),
             pltpu.VMEM((3, 2, FACE, LO), F32),
@@ -450,7 +571,7 @@
             collective_id=0, has_side_effects=True, vmem_limit_bytes=48 * 2**20
         ),
         name="exchange_stage",
-    )(ext, lo_ids, q_ids, face_lo, face_q, scale, mass_pair)
+    )(ext, lo_ids, q_ids, scale, send_up, send_down, jnp.asarray(mass_pair))
 
     out = jax.ShapeDtypeStruct((TR, NODE_DEV), F32)
     return pl.pallas_call(

time: 88.1 us -> 75.5 us (0.86)
  Pallas kernels: 79.6 us -> 68.1 us
  other arithmetic: 1.49 us -> 0 us
    pallas_call x1, Pallas kernels: 51.4 us -> 44.1 us  [per_device(): pl.pallas_call(functools.partial(exchange_kernel, n), out_shape=(field, f...]
    pallas_call x1, Pallas kernels: 19.6 us -> 16.4 us  [per_device(): pl.pallas_call(pair_kernel, out_shape=(jax.ShapeDtypeStruct((Q_ALL * TR,...]
    unnamed x10 -> x19, local copies, waits for them, and re-layouts: 3.99 us -> 6.27 us
    unnamed x2 -> x0, other arithmetic: 1.44 us -> none
    reshape x2 -> x0, local copies, waits for them, and re-layouts: 1.07 us -> none  [per_device(): connectivity.reshape(elements, NP // 2, 2).transpose(0, 2, 1)]
    pallas_call x1, Pallas kernels: 8.55 us -> 7.63 us  [per_device(): pl.pallas_call(output_kernel, out_shape=(out, out, out), in_specs=[vmem]...]
    broadcast_in_dim x3 -> x0, local copies, waits for them, and re-layouts: 0.9 us -> none  [per_device(): scale = jnp.repeat(jacobian, NP).reshape(chunks, CHUNK)]
where the time goes in v2:
time: 75.5 us; the launch traced here: 75.1 us
  Pallas kernels  68.1 us (90%)
  local copies, waits for them, and re-layouts  6.27 us (8%)
    pallas_call x1, Pallas kernels, per_device(): pl.pallas_call(functools.partial(exchange_kernel, n), out_shape=(field, f...  44.1 us
    pallas_call x1, Pallas kernels, per_device(): pl.pallas_call(pair_kernel, out_shape=(jax.ShapeDtypeStruct((Q_ALL * TR,...  16.4 us
    pallas_call x1, Pallas kernels, per_device(): pl.pallas_call(output_kernel, out_shape=(out, out, out), in_specs=[vmem]...  7.63 us
    unnamed x19, local copies, waits for them, and re-layouts  6.27 us

profile of v2, /device:TPU:0, one launch (start us, length us, event | category | flops | bytes accessed | tf_op | source)
XLA Modules:
  0.0 75.1 jit_solution(14464169725497747144)
XLA Ops:
  0.6 0.0 copy-start.4
  0.6 0.0 copy-start.5
  0.7 0.9 %copy.13.slots_ref = s32[128,64]{1,0:T(8,128)S(1)} copy(s32[128,64]{0,1:T(8,128)} %param.10) | data formatting | bytes 65536 | tf_op args[0]
  1.5 0.0 copy-start
  1.5 1.6 %copy-done = bf16[256,4096]{1,0:T(8,128)(2,1)S(1)} copy-done((bf16[256,4096]{1,0:T(8,128)(2,1)S(1)}, bf16[256,4096]{1,0:T(8,128)(2,1)}, u32[]{:S(2)}) %copy-start) | copy-done | bytes 2097176
  3.1 0.0 copy-start.1
  3.1 1.0 %copy-done.1 = bf16[32,8192]{1,0:T(8,128)(2,1)S(1)} copy-done((bf16[32,8192]{1,0:T(8,128)(2,1)S(1)}, bf16[32,8192]{1,0:T(8,128)(2,1)}, u32[]{:S(2)}) %copy-start.1) | copy-done | bytes 524312
  4.2 0.0 copy-start.3
  4.2 0.8 %copy-done.3 = f32[64,128]{1,0:T(8,128)S(1)} copy-done((f32[64,128]{1,0:T(8,128)S(1)}, f32[64,128]{1,0:T(8,128)}, u32[]{:S(2)}) %copy-start.3) | copy-done | bytes 32792
  4.9 0.0 copy-start.6
  4.9 0.7 copy-done.6
  5.6 0.0 copy-start.7
  5.6 0.7 copy-done.7
  6.3 0.0 copy-start.8
  6.3 0.7 copy-done.8
  6.9 0.0 copy-start.2
  6.9 16.4 %pair_stage.1 = (f32[416,384]{1,0:T(8,128)S(1)}, s32[16,512]{1,0:T(8,128)S(1)}, s32[16,512]{1,0:T(8,128)S(1)}, f32[16,512]{1,0:T(8,128)S(1)}) custom-call(s32[256]{0:T(256)S(1)} %copy-done.6, s32[256]{0:T(256)S(1)} %copy-done.7, bf16[256,4096]{1,0:T(8,128)(2,1)S(1)} %copy-done, bf16[32,8192]{1,0:T(8,128)(2,1)S(1)} %copy-done.1, ...), custom_call_target="tpu_custom_call" | custom-call | tf_op jit(solution)/shard_map/pair_stage/pallas_call | solution.py:514
  23.4 0.0 copy-done.4
  23.4 0.0 copy-done.5
  23.4 0.0 copy-done.2
  23.4 44.1 %exchange_stage.1 = (f32[32,3456]{1,0:T(8,128)S(1)}, f32[32,3456]{1,0:T(8,128)S(1)}, f32[32,128]{1,0:T(8,128)S(1)}) custom-call(f32[416,384]{1,0:T(8,128)S(1)} %get-tuple-element.10.ext_ref, s32[16,512]{1,0:T(8,128)S(1)} %get-tuple-element.11.lo_ref, s32[16,512]{1,0:T(8,128)S(1)} %get-tuple-element.12.q_ref, f32[16,512]{1,0:T(8,128)S(1)} %get-tuple-element.13.scale_ref, ...), custom_call_target="tpu_custom_call" | custom-call | tf_op jit(solution)/shard_map/exchange_stage/pallas_call | solution.py:547
  67.5 7.6 %output_stage.1 = (f32[32,3456]{1,0:T(8,128)}, f32[32,3456]{1,0:T(8,128)}, f32[32,3456]{1,0:T(8,128)}) custom-call(f32[32,128]{1,0:T(8,128)S(1)} %get-tuple-element.14.gram_ref, f32[32,3456]{1,0:T(8,128)S(1)} %get-tuple-element.15.right_ref, f32[32,3456]{1,0:T(8,128)S(1)} %get-tuple-element.16.image_ref), custom_call_target="tpu_custom_call" | custom-call | tf_op jit(solution)/shard_map/output_stage/pallas_call | solution.py:577
Async XLA Ops:
  0.6 22.7 %copy-start.4 = (s32[1,768]{1,0:T(1,128)S(1)}, s32[1,768]{1,0:T(1,128)}, u32[]{:S(2)}) copy-start(s32[1,768]{1,0:T(1,128)} %up_ref.1) | copy-start | bytes 9220
  0.6 22.7 %copy-start.5 = (s32[1,768]{1,0:T(1,128)S(1)}, s32[1,768]{1,0:T(1,128)}, u32[]{:S(2)}) copy-start(s32[1,768]{1,0:T(1,128)} %down_ref.1) | copy-start | bytes 9220
  1.5 1.6 %copy-start = (bf16[256,4096]{1,0:T(8,128)(2,1)S(1)}, bf16[256,4096]{1,0:T(8,128)(2,1)}, u32[]{:S(2)}) copy-start(bf16[256,4096]{1,0:T(8,128)(2,1)} %blocks_hbm.1) | copy-start | bytes 6291460
  3.1 1.0 %copy-start.1 = (bf16[32,8192]{1,0:T(8,128)(2,1)S(1)}, bf16[32,8192]{1,0:T(8,128)(2,1)}, u32[]{:S(2)}) copy-start(bf16[32,8192]{1,0:T(8,128)(2,1)} %values_ref.1) | copy-start | bytes 1572868
  4.2 0.8 %copy-start.3 = (f32[64,128]{1,0:T(8,128)S(1)}, f32[64,128]{1,0:T(8,128)}, u32[]{:S(2)}) copy-start(f32[64,128]{1,0:T(8,128)} %constant.4.clone.order_ref) | copy-start | bytes 98308
  4.9 0.7 copy-start.6
  5.6 0.7 copy-start.7
  6.3 0.7 copy-start.8
  6.9 16.5 %copy-start.2 = (bf16[2,256,256]{2,1,0:T(8,128)(2,1)S(1)}, bf16[2,256,256]{2,1,0:T(8,128)(2,1)}, u32[]{:S(2)}) copy-start(bf16[2,256,256]{2,1,0:T(8,128)(2,1)} %constant.5.clone.mass_ref) | copy-start | bytes 786436

commit v3 on v2

--- a/solution.py
+++ b/solution.py
@@ -2,8 +2,6 @@
 
 import jax
 import jax.numpy as jnp
-import ml_dtypes
-import numpy as np
 from jax import lax
 from jax.experimental import pallas as pl
 from jax.experimental.pallas import tpu as pltpu
@@ -27,25 +25,30 @@
 BF16 = jnp.bfloat16
 NT = (((1,), (1,)), ((), ()))
 
-line_mass = (
-    np.array(
-        [
-            [128.0, 99.0, -36.0, 19.0],
-            [99.0, 648.0, -81.0, -36.0],
-            [-36.0, -81.0, 648.0, 99.0],
-            [19.0, -36.0, 99.0, 128.0],
-        ]
-    )
-    / 504.0
-)
-mass_table = np.kron(np.kron(line_mass, line_mass), line_mass)
-node_order = np.arange(NP).reshape(NP // 2, 2).T.reshape(-1)
-mass_block = np.kron(np.eye(4), mass_table[np.ix_(node_order, node_order)]).astype(np.float32)
-mass_first = mass_block.astype(ml_dtypes.bfloat16)
-mass_pair = np.stack(
-    [mass_first, (mass_block - mass_first.astype(np.float32)).astype(ml_dtypes.bfloat16)]
-)
-order_table = np.tile(np.eye(NP, dtype=np.float32)[:, node_order], (1, 2))
+
+def line_entry(a, b):
+    apart = jnp.abs(a - b)
+    inner = jnp.logical_or(a == 1, a == 2)
+    near = jnp.where(a + b == 3, -81.0, 99.0)
+    far = jnp.where(apart == 2, -36.0, 19.0)
+    return jnp.where(apart == 0, jnp.where(inner, 648.0, 128.0), jnp.where(apart == 1, near, far))
+
+
+def node_of(position):
+    return jnp.bitwise_and(position, 31) * 2 + jnp.bitwise_and(jnp.right_shift(position, 5), 1)
+
+
+def mass_block():
+    shape = (4 * NP, 4 * NP)
+    rows, columns = lax.broadcasted_iota(jnp.int32, shape, 0), lane_ids(shape)
+    first, second = node_of(rows), node_of(columns)
+    value = jnp.where(jnp.right_shift(rows, 6) == jnp.right_shift(columns, 6), 504.0**-3, 0.0)
+    for digit in (0, 2, 4):
+        value = value * line_entry(
+            jnp.bitwise_and(jnp.right_shift(first, digit), 3),
+            jnp.bitwise_and(jnp.right_shift(second, digit), 3),
+        )
+    return value
 
 
 def lane_ids(shape):
@@ -63,25 +66,40 @@
     return jnp.where(rows == lo_row, 1.0, 0.0).astype(BF16)
 
 
-def spread(both, q_both, blocks):
+def stacked(value):
+    return jnp.concatenate(pieces(value), axis=0)
+
+
+def spread(stack, q_row, blocks):
     return jnp.concatenate(
-        [both * jnp.where(q_both == q, 1.0, 0.0).astype(BF16) for q in blocks], axis=0
+        [stack * jnp.where(q_row == q, 1.0, 0.0).astype(BF16) for q in blocks], axis=0
     )
-
-
-def twice(value, axis):
-    return jnp.concatenate([value, value], axis=axis)
 
 
 def add_up(left, right):
     return lax.dot_general(left, right, NT, preferred_element_type=F32)
 
 
+def joined(value):
+    return jnp.concatenate(
+        [
+            value[at : at + TR] + value[at + TR : at + 2 * TR]
+            for at in range(0, value.shape[0], 2 * TR)
+        ],
+        axis=0,
+    )
+
+
+def scatter(stack, q_row, blocks, hot):
+    return joined(add_up(spread(stack, q_row, blocks), hot))
+
+
 def gather(table, q_row, blocks, hot):
-    found = jnp.dot(table, twice(hot, 0), preferred_element_type=F32)
+    found = jnp.dot(table, hot, preferred_element_type=F32)
     total = None
     for at, q in enumerate(blocks):
-        part = jnp.where(q_row == q, found[at * TR : (at + 1) * TR], 0.0)
+        rows = found[2 * at * TR : (2 * at + 2) * TR]
+        part = jnp.where(q_row == q, rows[0:TR] + rows[TR:], 0.0)
         total = part if total is None else total + part
     return total
 
@@ -98,11 +116,14 @@
     values_ref,
     slots_ref,
     jacobian_ref,
-    order_ref,
+    up_ref,
+    down_ref,
     out_ref,
     lo_ref,
     q_ref,
     scale_ref,
+    face_lo_ref,
+    face_q_ref,
     blocks_ref,
     flat,
     table,
@@ -133,8 +154,13 @@
             axis=1,
         )
 
+    shape = (NP, 2 * NP)
+    order = lax.broadcasted_iota(jnp.int32, shape, 0) == node_of(lane_ids(shape))
     wide[...] = jnp.dot(
-        slots_ref[...].astype(F32), order_ref[...], precision=HIGH, preferred_element_type=F32
+        slots_ref[...].astype(F32),
+        jnp.where(order, 1.0, 0.0),
+        precision=HIGH,
+        preferred_element_type=F32,
     )
     q_ids, lo_ids = split_slots((by_chunk() + 0.5).astype(jnp.int32))
     q_ref[...] = q_ids
@@ -147,6 +173,10 @@
         preferred_element_type=F32,
     )
     scale_ref[...] = by_chunk()
+    for way, face_ref in enumerate((up_ref, down_ref)):
+        q_ids, lo_ids = split_slots(face_ref[...])
+        face_q_ref[way : way + 1, :] = q_ids
+        face_lo_ref[way : way + 1, :] = lo_ids
 
     for w in range(elements // 2):
         window = values_ref[:, w * 128 : (w + 1) * 128].astype(F32)
@@ -154,7 +184,6 @@
         table[2 * w] = jnp.where(lanes < 64, window, turned).astype(BF16)
         table[2 * w + 1] = jnp.where(lanes < 64, turned, window).astype(BF16)
     total[...] = jnp.zeros_like(total)
-    out_ref[...] = jnp.zeros_like(out_ref)
     fetch.wait()
 
     def lay_out(g, carry):
@@ -191,10 +220,7 @@
             tiles.append(
                 jnp.where(lanes < 64, even + pltpu.roll(even, 64, 1), odd + pltpu.roll(odd, 64, 1))
             )
-        both = jnp.concatenate(pieces(jnp.concatenate(tiles, axis=1)), axis=1)
-        q_both = twice(q_ref[pl.ds(step, 1), :], 1)
-        hot = one_hot(lo_ref[pl.ds(step, 1), :])
-        out_ref[...] += add_up(spread(both, q_both, range(Q_ALL)), twice(hot, 1))
+        out_ref[step] = stacked(jnp.concatenate(tiles, axis=1))
         return carry
 
     lax.fori_loop(0, chunks, add, 0, unroll=2)
@@ -202,17 +228,17 @@
 
 def exchange_kernel(
     n,
-    ext_ref,
+    sums_ref,
     lo_ref,
     q_ref,
     scale_ref,
-    up_ref,
-    down_ref,
-    mass_ref,
+    face_lo_ref,
+    face_q_ref,
     right_ref,
     image_ref,
     gram_ref,
     table,
+    mass,
     hot,
     face_hot,
     found,
@@ -251,17 +277,6 @@
     def _():
         pl.semaphore_signal(barrier, inc=1, device_id=(me - 1,), device_id_type=MESH)
 
-    partners = group + layers - 2
-    crossing = jnp.logical_or(cross_up, cross_down)
-
-    @pl.when(crossing)
-    def _():
-        pl.semaphore_wait(barrier, partners + 1)
-
-    @pl.when(jnp.logical_not(crossing))
-    def _():
-        pl.semaphore_wait(barrier, partners)
-
     def copy(source, phase, way):
         return pltpu.make_async_remote_copy(
             src_ref=source,
@@ -295,105 +310,123 @@
     up_rows = pl.ds(OWN + FACE, FACE)
     own_blocks, face_blocks = range(Q_OWN), range(Q_OWN, Q_ALL)
     chunks = lo_ref.shape[0]
-
-    start(ext_ref.at[down_rows], 0, 0)
-    start(ext_ref.at[up_rows], 0, 1)
-
-    def mark(step, carry):
-        hot[step] = one_hot(lo_ref[pl.ds(step, 1), :])
+    ext[...] = jnp.zeros_like(ext)
+
+    def fill(rows, value):
+        first, second = pieces(value)
+        for b in range(value.shape[0] // TR):
+            at = (rows + b) * 2 * TR
+            table[at : at + TR] = first[b * TR : (b + 1) * TR]
+            table[at + TR : at + 2 * TR] = second[b * TR : (b + 1) * TR]
+
+    def face_sums(step, carry):
+        marks = one_hot(lo_ref[pl.ds(step, 1), :])
+        hot[step] = marks
+        ext[0, OWN:, :] += scatter(sums_ref[step], q_ref[pl.ds(step, 1), :], face_blocks, marks)
         return carry
 
-    lax.fori_loop(0, chunks, mark, 0)
-    faces = [split_slots(up_ref[...]), split_slots(down_ref[...])]
+    lax.fori_loop(0, chunks, face_sums, 0, unroll=2)
+    partners = group + layers - 2
+    crossing = jnp.logical_or(cross_up, cross_down)
+
+    @pl.when(crossing)
+    def _():
+        pl.semaphore_wait(barrier, partners + 1)
+
+    @pl.when(jnp.logical_not(crossing))
+    def _():
+        pl.semaphore_wait(barrier, partners)
+
+    start(ext.at[0, down_rows], 0, 0)
+    start(ext.at[0, up_rows], 0, 1)
+
+    def own_sums(values, phase):
+        def step_sums(step, carry):
+            ext[phase, 0:OWN, :] += scatter(
+                values[step], q_ref[pl.ds(step, 1), :], own_blocks, hot[step]
+            )
+            return carry
+
+        lax.fori_loop(0, chunks, step_sums, 0, unroll=2)
+
+    own_sums(sums_ref, 0)
     for way in range(2):
-        face_hot[way] = one_hot(faces[way][1])
+        face_hot[:, way * F : (way + 1) * F] = one_hot(face_lo_ref[way : way + 1, :])
+    first, second = pieces(mass_block())
+    mass[0] = first
+    mass[1] = second
 
     def settle(own, phase):
-        left, right = [], []
+        left = []
         for way in range(2):
             for b in range(Q_FACE):
                 part = slice(b * LO, (b + 1) * LO)
-                both = jnp.concatenate(
-                    pieces(incoming[phase, way, b * TR : (b + 1) * TR, :]), axis=1
-                )
-                left.append(spread(both, twice(faces[way][0][:, part], 1), own_blocks))
-                right.append(twice(face_hot[way, :, part], 1))
-        return own + add_up(jnp.concatenate(left, axis=1), jnp.concatenate(right, axis=1))
-
-    arrive(ext_ref.at[down_rows], 0, 0)
-    arrive(ext_ref.at[up_rows], 0, 1)
-    right = settle(ext_ref[0:OWN, :], 0)
-    first, second = pieces(right)
-    table[0:OWN, 0:LO] = first
-    table[0:OWN, LO : 2 * LO] = second
-
+                stack = stacked(incoming[phase, way, b * TR : (b + 1) * TR, :])
+                left.append(spread(stack, face_q_ref[way : way + 1, part], own_blocks))
+        return own + joined(add_up(jnp.concatenate(left, axis=1), face_hot[...]))
+
+    arrive(ext.at[0, down_rows], 0, 0)
+    arrive(ext.at[0, up_rows], 0, 1)
+    right = settle(ext[0, 0:OWN, :], 0)
+    fill(0, right)
+
+    own_table, face_table = pl.ds(0, 2 * OWN), pl.ds(2 * OWN, 4 * FACE)
     for way in (1, 0):
-        values = gather(table[0:OWN, :], faces[1 - way][0], own_blocks, face_hot[1 - way])
+        mine = slice((1 - way) * F, (2 - way) * F)
+        values = gather(
+            table[own_table, :], face_q_ref[1 - way : 2 - way, :], own_blocks, face_hot[:, mine]
+        )
         for b in range(Q_FACE):
             outgoing[way, b * TR : (b + 1) * TR, :] = values[:, b * LO : (b + 1) * LO]
         start(outgoing.at[way], 1, way)
 
     def own_values(step, carry):
         q_row = q_ref[pl.ds(step, 1), :]
-        found[step] = gather(table[0:OWN, :], q_row, own_blocks, hot[step])
+        found[step] = gather(table[own_table, :], q_row, own_blocks, hot[step])
         return carry
 
     lax.fori_loop(0, chunks, own_values, 0, unroll=2)
     for q in own_blocks:
         right_ref[:, q * LO : (q + 1) * LO] = right[q * TR : (q + 1) * TR]
-    ext[...] = jnp.zeros_like(ext)
     for way in (1, 0):
         arrive(outgoing.at[way], 1, way)
-        rows = OWN if way else OWN + FACE
-        first, second = pieces(incoming[1, way])
-        table[rows : rows + FACE, 0:LO] = first
-        table[rows : rows + FACE, LO : 2 * LO] = second
+        fill(Q_OWN if way else Q_OWN + Q_FACE, incoming[1, way])
 
     def elements(step, carry):
         q_row = q_ref[pl.ds(step, 1), :]
-        values = found[step] + gather(table[OWN:, :], q_row, face_blocks, hot[step])
+        values = found[step] + gather(table[face_table, :], q_row, face_blocks, hot[step])
         first, second = pieces(
             jnp.concatenate([values[:, h : h + 256] for h in range(0, CHUNK, 256)], axis=0)
         )
         result = (
-            jnp.dot(first, mass_ref[0], preferred_element_type=F32)
-            + jnp.dot(second, mass_ref[0], preferred_element_type=F32)
-            + jnp.dot(first, mass_ref[1], preferred_element_type=F32)
+            jnp.dot(first, mass[0], preferred_element_type=F32)
+            + jnp.dot(second, mass[0], preferred_element_type=F32)
+            + jnp.dot(first, mass[1], preferred_element_type=F32)
         )
         result = jnp.concatenate(
             [result[h * TR : (h + 1) * TR] for h in range(CHUNK // 256)], axis=1
         )
-        both = jnp.concatenate(pieces(result * scale_ref[pl.ds(step, 1), :]), axis=1)
-        applied[step] = both
-        ext[OWN:, :] += add_up(spread(both, twice(q_row, 1), face_blocks), twice(hot[step], 1))
+        stack = stacked(result * scale_ref[pl.ds(step, 1), :])
+        applied[step] = stack
+        ext[1, OWN:, :] += scatter(stack, q_row, face_blocks, hot[step])
         return carry
 
     lax.fori_loop(0, chunks, elements, 0, unroll=2)
-    start(ext.at[down_rows], 2, 0)
-    start(ext.at[up_rows], 2, 1)
-
-    def own_sums(step, carry):
-        q_both = twice(q_ref[pl.ds(step, 1), :], 1)
-        ext[0:OWN, :] += add_up(spread(applied[step], q_both, own_blocks), twice(hot[step], 1))
-        return carry
-
-    lax.fori_loop(0, chunks, own_sums, 0, unroll=2)
-    arrive(ext.at[down_rows], 2, 0)
-    arrive(ext.at[up_rows], 2, 1)
-    image = settle(ext[0:OWN, :], 2)
+    start(ext.at[1, down_rows], 2, 0)
+    start(ext.at[1, up_rows], 2, 1)
+    own_sums(applied, 1)
+    arrive(ext.at[1, down_rows], 2, 0)
+    arrive(ext.at[1, up_rows], 2, 1)
+    image = settle(ext[1, 0:OWN, :], 2)
     for q in own_blocks:
         image_ref[:, q * LO : (q + 1) * LO] = image[q * TR : (q + 1) * TR]
 
-    def as_row(value):
-        return jnp.concatenate([value[q * TR : (q + 1) * TR] for q in own_blocks], axis=1)
-
-    first, second = pieces(image)
     stack = jnp.concatenate(
         [
-            as_row(table[0:OWN, 0:LO]),
-            as_row(table[0:OWN, LO : 2 * LO]),
-            as_row(first),
-            as_row(second),
+            jnp.concatenate([table[q * 2 * TR : (q + 1) * 2 * TR, :] for q in own_blocks], axis=1),
+            jnp.concatenate(
+                [stacked(image[q * TR : (q + 1) * TR]) for q in own_blocks], axis=1
+            ),
         ],
         axis=0,
     )
@@ -430,12 +463,12 @@
     gram = sum_over(gram, near, near_ids, near_send, near_recv)
     gram_ref[...] = sum_over(gram, far, far_ids, far_send, far_recv)
 
-    finish(ext_ref.at[down_rows], 0, 0)
-    finish(ext_ref.at[up_rows], 0, 1)
+    finish(ext.at[0, down_rows], 0, 0)
+    finish(ext.at[0, up_rows], 0, 1)
     for way in range(2):
         finish(outgoing.at[way], 1, way)
-    finish(ext.at[down_rows], 2, 0)
-    finish(ext.at[up_rows], 2, 1)
+    finish(ext.at[1, down_rows], 2, 0)
+    finish(ext.at[1, up_rows], 2, 1)
 
 
 def output_kernel(gram_ref, right_ref, image_ref, solution_ref, residual_ref, basis_ref):
@@ -511,16 +544,19 @@
     smem = pl.BlockSpec(memory_space=pltpu.SMEM)
 
     ids = jax.ShapeDtypeStruct((chunks, CHUNK), jnp.int32)
-    ext, lo_ids, q_ids, scale = pl.pallas_call(
+    face_ids = jax.ShapeDtypeStruct((2, F), jnp.int32)
+    prepared = pl.pallas_call(
         pair_kernel,
         out_shape=(
-            jax.ShapeDtypeStruct((Q_ALL * TR, LO), F32),
+            jax.ShapeDtypeStruct((chunks, 2 * TR, CHUNK), BF16),
             ids,
             ids,
             jax.ShapeDtypeStruct((chunks, CHUNK), F32),
+            face_ids,
+            face_ids,
         ),
-        in_specs=[smem, smem, pl.BlockSpec(memory_space=pl.ANY), vmem, vmem, vmem, vmem],
-        out_specs=(vmem,) * 4,
+        in_specs=[smem, smem, pl.BlockSpec(memory_space=pl.ANY)] + [vmem] * 5,
+        out_specs=(vmem,) * 6,
         scratch_shapes=[
             pltpu.VMEM(pair_blocks.shape, BF16),
             pltpu.VMEM((pairs * 32, 128), F32),
@@ -529,7 +565,7 @@
             pltpu.VMEM((elements, 128), F32),
             pltpu.SemaphoreType.DMA,
         ],
-        compiler_params=pltpu.CompilerParams(vmem_limit_bytes=48 * 2**20),
+        compiler_params=pltpu.CompilerParams(vmem_limit_bytes=61 * 2**20),
         name="pair_stage",
     )(
         pair_target,
@@ -538,7 +574,8 @@
         source_values,
         connectivity,
         jacobian.reshape(1, elements),
-        jnp.asarray(order_table),
+        send_up,
+        send_down,
     )
 
     group = min(GROUP, n)
@@ -547,15 +584,16 @@
     right, image, gram = pl.pallas_call(
         functools.partial(exchange_kernel, n),
         out_shape=(field, field, jax.ShapeDtypeStruct((TR, 128), F32)),
-        in_specs=[vmem] * 7,
+        in_specs=[vmem] * 6,
         out_specs=(vmem, vmem, vmem),
         scratch_shapes=[
-            pltpu.VMEM((Q_ALL * TR, 2 * LO), BF16),
+            pltpu.VMEM((Q_ALL * 2 * TR, LO), BF16),
+            pltpu.VMEM((2, 4 * NP, 4 * NP), BF16),
             pltpu.VMEM((chunks, LO, CHUNK), BF16),
-            pltpu.VMEM((2, LO, F), BF16),
+            pltpu.VMEM((LO, 2 * F), BF16),
             pltpu.VMEM((chunks, TR, CHUNK), F32),
-            pltpu.VMEM((chunks, TR, 2 * CHUNK), BF16),
-            pltpu.VMEM((Q_ALL * TR, LO), F32),
+            pltpu.VMEM((chunks, 2 * TR, CHUNK), BF16),
+            pltpu.VMEM((2, Q_ALL * TR, LO), F32),
             pltpu.VMEM((2, FACE, LO), F32),
             pltpu.VMEM((3, 2, FACE, LO), F32),
             pltpu.VMEM((group, TR, 128), F32),
@@ -571,7 +609,7 @@
             collective_id=0, has_side_effects=True, vmem_limit_bytes=48 * 2**20
         ),
         name="exchange_stage",
-    )(ext, lo_ids, q_ids, scale, send_up, send_down, jnp.asarray(mass_pair))
+    )(*prepared)
 
     out = jax.ShapeDtypeStruct((TR, NODE_DEV), F32)
     return pl.pallas_call(

time: 75.5 us -> 78.2 us (1.036)
  Pallas kernels: 68.1 us -> 70.6 us
    pallas_call x1, Pallas kernels: 44.1 us -> 52.2 us  [per_device(): pl.pallas_call(functools.partial(exchange_kernel, n), out_shape=(field, f...]
    pallas_call x1, Pallas kernels: 16.4 us -> 10.8 us  [per_device(): pl.pallas_call(pair_kernel, out_shape=(jax.ShapeDtypeStruct((chunks, 2 *...]
    unnamed x19 -> x13, local copies, waits for them, and re-layouts: 6.27 us -> 6.36 us
where the time goes in v3:
time: 78.2 us; the launch traced here: 77.7 us
  Pallas kernels  70.6 us (90%)
  local copies, waits for them, and re-layouts  6.36 us (8%)
    pallas_call x1, Pallas kernels, per_device(): pl.pallas_call(functools.partial(exchange_kernel, n), out_shape=(field, f...  52.2 us
    pallas_call x1, Pallas kernels, per_device(): pl.pallas_call(pair_kernel, out_shape=(jax.ShapeDtypeStruct((chunks, 2 *...  10.8 us
    pallas_call x1, Pallas kernels, per_device(): pl.pallas_call(output_kernel, out_shape=(out, out, out), in_specs=[vmem]...  7.63 us
    unnamed x13, local copies, waits for them, and re-layouts  6.36 us

profile of v3, /device:TPU:0, one launch (start us, length us, event | category | flops | bytes accessed | tf_op | source)
XLA Modules:
  0.0 77.7 jit_solution(12863079921185747391)
XLA Ops:
  0.6 1.5 %copy.11.slots_ref = s32[128,64]{1,0:T(8,128)} copy(s32[128,64]{0,1:T(8,128)} %param.8) | data formatting | bytes 65536 | tf_op args[0]
  2.1 10.8 %pair_stage.1 = (bf16[16,64,512]{2,1,0:T(8,128)(2,1)}, s32[16,512]{1,0:T(8,128)}, s32[16,512]{1,0:T(8,128)}, f32[16,512]{1,0:T(8,128)}, s32[2,768]{1,0:T(2,128)}, /*index=5*/s32[2,768]{1,0:T(2,128)}) custom-call(s32[256]{0:T(256)} %target_ref.1, s32[256]{0:T(256)} %source_ref.1, bf16[256,4096]{1,0:T(8,128)(2,1)} %blocks_hbm.1, bf16[32,8192]{1,0:T(8,128)(2,1)} %values_ref.1, ...), custom_call_target="tpu_custom_call" | custom-call | tf_op jit(solution)/shard_map/pair_stage/pallas_call | solution.py:548
  13.0 0.0 copy-start
  13.0 1.2 %copy-done = bf16[16,64,512]{2,1,0:T(8,128)(2,1)S(1)} copy-done((bf16[16,64,512]{2,1,0:T(8,128)(2,1)S(1)}, bf16[16,64,512]{2,1,0:T(8,128)(2,1)}, u32[]{:S(2)}) %copy-start) | copy-done | bytes 1048600
  14.2 0.0 copy-start.1
  14.2 0.8 copy-done.1
  15.0 0.0 copy-start.2
  15.0 0.8 copy-done.2
  15.7 0.0 copy-start.3
  15.7 0.8 copy-done.3
  16.5 0.0 copy-start.4
  16.5 0.7 copy-done.4
  17.2 0.0 copy-start.5
  17.2 0.7 copy-done.5
  17.9 52.2 %exchange_stage.1 = (f32[32,3456]{1,0:T(8,128)S(1)}, f32[32,3456]{1,0:T(8,128)S(1)}, f32[32,128]{1,0:T(8,128)S(1)}) custom-call(bf16[16,64,512]{2,1,0:T(8,128)(2,1)S(1)} %copy-done, s32[16,512]{1,0:T(8,128)S(1)} %copy-done.1, s32[16,512]{1,0:T(8,128)S(1)} %copy-done.2, f32[16,512]{1,0:T(8,128)S(1)} %copy-done.3, s32[2,768]{1,0:T(2,128)S(1)} %copy-done.4, ...), custom_call_target="tpu_custom_call" | custom-call | tf_op jit(solution)/shard_map/exchange_stage/pallas_call | solution.py:584
  70.0 7.6 %output_stage.1 = (f32[32,3456]{1,0:T(8,128)}, f32[32,3456]{1,0:T(8,128)}, f32[32,3456]{1,0:T(8,128)}) custom-call(f32[32,128]{1,0:T(8,128)S(1)} %get-tuple-element.18.gram_ref, f32[32,3456]{1,0:T(8,128)S(1)} %get-tuple-element.19.right_ref, f32[32,3456]{1,0:T(8,128)S(1)} %get-tuple-element.20.image_ref), custom_call_target="tpu_custom_call" | custom-call | tf_op jit(solution)/shard_map/output_stage/pallas_call | solution.py:615
Async XLA Ops:
  13.0 1.2 %copy-start = (bf16[16,64,512]{2,1,0:T(8,128)(2,1)S(1)}, bf16[16,64,512]{2,1,0:T(8,128)(2,1)}, u32[]{:S(2)}) copy-start(bf16[16,64,512]{2,1,0:T(8,128)(2,1)} %get-tuple-element.12.sums_ref) | copy-start | bytes 3145732
  14.2 0.8 copy-start.1
  15.0 0.8 copy-start.2
  15.7 0.8 copy-start.3
  16.5 0.7 copy-start.4
  17.2 0.7 copy-start.5

commit v4 on v3

--- a/solution.py
+++ b/solution.py
@@ -94,14 +94,19 @@
     return joined(add_up(spread(stack, q_row, blocks), hot))
 
 
-def gather(table, q_row, blocks, hot):
-    found = jnp.dot(table, hot, preferred_element_type=F32)
-    total = None
-    for at, q in enumerate(blocks):
-        rows = found[2 * at * TR : (2 * at + 2) * TR]
-        part = jnp.where(q_row == q, rows[0:TR] + rows[TR:], 0.0)
-        total = part if total is None else total + part
-    return total
+def gather(table, first_tile, tiles, q_row, lo_row):
+    tile_row = q_row * (LO // 128) + jnp.right_shift(lo_row, 7)
+    lane_row = jnp.bitwise_and(lo_row, 127)
+    columns = []
+    for at in range(0, q_row.shape[1], 128):
+        tile = jnp.broadcast_to(tile_row[:, at : at + 128], (TR, 128))
+        lane = jnp.broadcast_to(lane_row[:, at : at + 128], (TR, 128))
+        total = jnp.zeros((TR, 128), F32)
+        for t in range(first_tile, first_tile + tiles):
+            here = jnp.take_along_axis(table[t * TR : (t + 1) * TR, :], lane, axis=1)
+            total = jnp.where(tile == t, here, total)
+        columns.append(total)
+    return jnp.concatenate(columns, axis=1)
 
 
 def split_slots(slots):
@@ -156,9 +161,10 @@
 
     shape = (NP, 2 * NP)
     order = lax.broadcasted_iota(jnp.int32, shape, 0) == node_of(lane_ids(shape))
-    wide[...] = jnp.dot(
+    wide[...] = lax.dot_general(
         slots_ref[...].astype(F32),
         jnp.where(order, 1.0, 0.0),
+        (((0,), (0,)), ((), ())),
         precision=HIGH,
         preferred_element_type=F32,
     )
@@ -312,12 +318,13 @@
     chunks = lo_ref.shape[0]
     ext[...] = jnp.zeros_like(ext)
 
-    def fill(rows, value):
-        first, second = pieces(value)
+    def fill(block, value):
         for b in range(value.shape[0] // TR):
-            at = (rows + b) * 2 * TR
-            table[at : at + TR] = first[b * TR : (b + 1) * TR]
-            table[at + TR : at + 2 * TR] = second[b * TR : (b + 1) * TR]
+            for part in range(LO // 128):
+                at = ((block + b) * (LO // 128) + part) * TR
+                table[at : at + TR, :] = value[
+                    b * TR : (b + 1) * TR, part * 128 : (part + 1) * 128
+                ]
 
     def face_sums(step, carry):
         marks = one_hot(lo_ref[pl.ds(step, 1), :])
@@ -370,22 +377,20 @@
     right = settle(ext[0, 0:OWN, :], 0)
     fill(0, right)
 
-    own_table, face_table = pl.ds(0, 2 * OWN), pl.ds(2 * OWN, 4 * FACE)
+    own_tiles, face_tiles = Q_OWN * LO // 128, 2 * F // 128
     for way in (1, 0):
-        mine = slice((1 - way) * F, (2 - way) * F)
-        values = gather(
-            table[own_table, :], face_q_ref[1 - way : 2 - way, :], own_blocks, face_hot[:, mine]
-        )
+        mine = slice(1 - way, 2 - way)
+        values = gather(table, 0, own_tiles, face_q_ref[mine, :], face_lo_ref[mine, :])
         for b in range(Q_FACE):
             outgoing[way, b * TR : (b + 1) * TR, :] = values[:, b * LO : (b + 1) * LO]
         start(outgoing.at[way], 1, way)
 
     def own_values(step, carry):
-        q_row = q_ref[pl.ds(step, 1), :]
-        found[step] = gather(table[own_table, :], q_row, own_blocks, hot[step])
+        q_row, lo_row = q_ref[pl.ds(step, 1), :], lo_ref[pl.ds(step, 1), :]
+        found[step] = gather(table, 0, own_tiles, q_row, lo_row)
         return carry
 
-    lax.fori_loop(0, chunks, own_values, 0, unroll=2)
+    lax.fori_loop(0, chunks, own_values, 0)
     for q in own_blocks:
         right_ref[:, q * LO : (q + 1) * LO] = right[q * TR : (q + 1) * TR]
     for way in (1, 0):
@@ -394,7 +399,8 @@
 
     def elements(step, carry):
         q_row = q_ref[pl.ds(step, 1), :]
-        values = found[step] + gather(table[face_table, :], q_row, face_blocks, hot[step])
+        lo_row = lo_ref[pl.ds(step, 1), :]
+        values = found[step] + gather(table, own_tiles, face_tiles, q_row, lo_row)
         first, second = pieces(
             jnp.concatenate([values[:, h : h + 256] for h in range(0, CHUNK, 256)], axis=0)
         )
@@ -423,10 +429,10 @@
 
     stack = jnp.concatenate(
         [
-            jnp.concatenate([table[q * 2 * TR : (q + 1) * 2 * TR, :] for q in own_blocks], axis=1),
             jnp.concatenate(
-                [stacked(image[q * TR : (q + 1) * TR]) for q in own_blocks], axis=1
-            ),
+                [stacked(field[q * TR : (q + 1) * TR]) for q in own_blocks], axis=1
+            )
+            for field in (right, image)
         ],
         axis=0,
     )
@@ -572,7 +578,7 @@
         pair_source,
         pair_blocks,
         source_values,
-        connectivity,
+        connectivity.T,
         jacobian.reshape(1, elements),
         send_up,
         send_down,
@@ -587,7 +593,7 @@
         in_specs=[vmem] * 6,
         out_specs=(vmem, vmem, vmem),
         scratch_shapes=[
-            pltpu.VMEM((Q_ALL * 2 * TR, LO), BF16),
+            pltpu.VMEM((Q_ALL * (LO // 128) * TR, 128), F32),
             pltpu.VMEM((2, 4 * NP, 4 * NP), BF16),
             pltpu.VMEM((chunks, LO, CHUNK), BF16),
             pltpu.VMEM((LO, 2 * F), BF16),
@@ -606,7 +612,7 @@
             pltpu.SemaphoreType.DMA((layers,)),
         ],
         compiler_params=pltpu.CompilerParams(
-            collective_id=0, has_side_effects=True, vmem_limit_bytes=48 * 2**20
+            collective_id=0, has_side_effects=True, vmem_limit_bytes=61 * 2**20
         ),
         name="exchange_stage",
     )(*prepared)
@@ -617,7 +623,7 @@
         out_shape=(out, out, out),
         in_specs=[vmem] * 3,
         out_specs=(vmem, vmem, vmem),
-        compiler_params=pltpu.CompilerParams(vmem_limit_bytes=32 * 2**20),
+        compiler_params=pltpu.CompilerParams(vmem_limit_bytes=61 * 2**20),
         name="output_stage",
     )(gram, right, image)
 

time: 78.2 us -> 77.1 us (0.986)
  local copies, waits for them, and re-layouts: 6.36 us -> 0 us
  Pallas kernels: 70.6 us -> 76.2 us
    unnamed x13 -> x0, local copies, waits for them, and re-layouts: 6.36 us -> none
    pallas_call x1, Pallas kernels: 52.2 us -> 56.6 us  [per_device(): pl.pallas_call(functools.partial(exchange_kernel, n), out_shape=(field, f...]
    pallas_call x1, Pallas kernels: 7.63 us -> 8.79 us  [per_device(): pl.pallas_call(output_kernel, out_shape=(out, out, out), in_specs=[vmem]...]
where the time goes in v4:
time: 77.1 us; the launch traced here: 76.9 us
  Pallas kernels  76.2 us (99%)
    pallas_call x1, Pallas kernels, per_device(): pl.pallas_call(functools.partial(exchange_kernel, n), out_shape=(field, f...  56.6 us
    pallas_call x1, Pallas kernels, per_device(): pl.pallas_call(pair_kernel, out_shape=(jax.ShapeDtypeStruct((chunks, 2 *...  10.8 us
    pallas_call x1, Pallas kernels, per_device(): pl.pallas_call(output_kernel, out_shape=(out, out, out), in_specs=[vmem]...  8.79 us

profile of v4, /device:TPU:0, one launch (start us, length us, event | category | flops | bytes accessed | tf_op | source)
XLA Modules:
  0.0 76.9 jit_solution(7720947096784825489)
XLA Ops:
  0.6 10.8 %pair_stage.1 = (bf16[16,64,512]{2,1,0:T(8,128)(2,1)}, s32[16,512]{1,0:T(8,128)}, s32[16,512]{1,0:T(8,128)}, f32[16,512]{1,0:T(8,128)}, s32[2,768]{1,0:T(2,128)}, /*index=5*/s32[2,768]{1,0:T(2,128)}) custom-call(s32[256]{0:T(256)} %target_ref.1, s32[256]{0:T(256)} %source_ref.1, bf16[256,4096]{1,0:T(8,128)(2,1)} %blocks_hbm.1, bf16[32,8192]{1,0:T(8,128)(2,1)} %values_ref.1, ...), custom_call_target="tpu_custom_call" | custom-call | tf_op jit(solution)/shard_map/pair_stage/pallas_call | solution.py:554
  11.5 56.6 %exchange_stage.1 = (f32[32,3456]{1,0:T(8,128)}, f32[32,3456]{1,0:T(8,128)}, f32[32,128]{1,0:T(8,128)}) custom-call(bf16[16,64,512]{2,1,0:T(8,128)(2,1)} %get-tuple-element.12.sums_ref, s32[16,512]{1,0:T(8,128)} %get-tuple-element.13.lo_ref, s32[16,512]{1,0:T(8,128)} %get-tuple-element.14.q_ref, f32[16,512]{1,0:T(8,128)} %get-tuple-element.15.scale_ref, ...), custom_call_target="tpu_custom_call" | custom-call | tf_op jit(solution)/shard_map/exchange_stage/pallas_call | solution.py:590
  68.1 8.8 %output_stage.1 = (f32[32,3456]{1,0:T(8,128)}, f32[32,3456]{1,0:T(8,128)}, f32[32,3456]{1,0:T(8,128)}) custom-call(f32[32,128]{1,0:T(8,128)} %get-tuple-element.18.gram_ref, f32[32,3456]{1,0:T(8,128)} %get-tuple-element.19.right_ref, f32[32,3456]{1,0:T(8,128)} %get-tuple-element.20.image_ref), custom_call_target="tpu_custom_call" | custom-call | tf_op jit(solution)/shard_map/output_stage/pallas_call | solution.py:621

commit v5 on v4

--- a/solution.py
+++ b/solution.py
@@ -18,6 +18,7 @@
 OWN = Q_OWN * TR
 FACE = Q_FACE * TR
 CHUNK = 512
+Q_PRODUCT = 5
 GROUP = 8
 MESH = pl.DeviceIdType.MESH
 HIGH = lax.Precision.HIGHEST
@@ -107,6 +108,16 @@
             total = jnp.where(tile == t, here, total)
         columns.append(total)
     return jnp.concatenate(columns, axis=1)
+
+
+def gather_product(table, blocks, q_row, hot):
+    found = jnp.dot(table, hot, preferred_element_type=F32)
+    total = None
+    for at, q in enumerate(blocks):
+        rows = found[2 * at * TR : (2 * at + 2) * TR]
+        part = jnp.where(q_row == q, rows[0:TR] + rows[TR:], 0.0)
+        total = part if total is None else total + part
+    return total
 
 
 def split_slots(slots):
@@ -244,6 +255,7 @@
     image_ref,
     gram_ref,
     table,
+    split_table,
     mass,
     hot,
     face_hot,
@@ -325,6 +337,10 @@
                 table[at : at + TR, :] = value[
                     b * TR : (b + 1) * TR, part * 128 : (part + 1) * 128
                 ]
+            if block + b < Q_PRODUCT:
+                split_table[(block + b) * 2 * TR : (block + b + 1) * 2 * TR, :] = stacked(
+                    value[b * TR : (b + 1) * TR]
+                )
 
     def face_sums(step, carry):
         marks = one_hot(lo_ref[pl.ds(step, 1), :])
@@ -378,29 +394,42 @@
     fill(0, right)
 
     own_tiles, face_tiles = Q_OWN * LO // 128, 2 * F // 128
+    first_tile = Q_PRODUCT * LO // 128
+
+    def own_gather(q_row, lo_row, marks):
+        return gather(table, first_tile, own_tiles - first_tile, q_row, lo_row) + gather_product(
+            split_table[...], range(Q_PRODUCT), q_row, marks
+        )
+
     for way in (1, 0):
         mine = slice(1 - way, 2 - way)
-        values = gather(table, 0, own_tiles, face_q_ref[mine, :], face_lo_ref[mine, :])
+        values = own_gather(
+            face_q_ref[mine, :], face_lo_ref[mine, :], face_hot[:, (1 - way) * F : (2 - way) * F]
+        )
         for b in range(Q_FACE):
             outgoing[way, b * TR : (b + 1) * TR, :] = values[:, b * LO : (b + 1) * LO]
         start(outgoing.at[way], 1, way)
 
     def own_values(step, carry):
         q_row, lo_row = q_ref[pl.ds(step, 1), :], lo_ref[pl.ds(step, 1), :]
-        found[step] = gather(table, 0, own_tiles, q_row, lo_row)
+        found[step] = own_gather(q_row, lo_row, hot[step])
         return carry
 
-    lax.fori_loop(0, chunks, own_values, 0)
+    lax.fori_loop(0, chunks, own_values, 0, unroll=2)
     for q in own_blocks:
         right_ref[:, q * LO : (q + 1) * LO] = right[q * TR : (q + 1) * TR]
     for way in (1, 0):
         arrive(outgoing.at[way], 1, way)
         fill(Q_OWN if way else Q_OWN + Q_FACE, incoming[1, way])
 
-    def elements(step, carry):
+    def face_values(step):
+        q_row, lo_row = q_ref[pl.ds(step, 1), :], lo_ref[pl.ds(step, 1), :]
+        return gather(table, own_tiles, face_tiles, q_row, lo_row)
+
+    def elements(step, from_faces):
         q_row = q_ref[pl.ds(step, 1), :]
-        lo_row = lo_ref[pl.ds(step, 1), :]
-        values = found[step] + gather(table, own_tiles, face_tiles, q_row, lo_row)
+        values = found[step] + from_faces
+        following = face_values(jnp.minimum(step + 1, chunks - 1))
         first, second = pieces(
             jnp.concatenate([values[:, h : h + 256] for h in range(0, CHUNK, 256)], axis=0)
         )
@@ -415,9 +444,9 @@
         stack = stacked(result * scale_ref[pl.ds(step, 1), :])
         applied[step] = stack
         ext[1, OWN:, :] += scatter(stack, q_row, face_blocks, hot[step])
-        return carry
-
-    lax.fori_loop(0, chunks, elements, 0, unroll=2)
+        return following
+
+    lax.fori_loop(0, chunks, elements, face_values(0), unroll=2)
     start(ext.at[1, down_rows], 2, 0)
     start(ext.at[1, up_rows], 2, 1)
     own_sums(applied, 1)
@@ -477,7 +506,18 @@
     finish(ext.at[1, up_rows], 2, 1)
 
 
-def output_kernel(gram_ref, right_ref, image_ref, solution_ref, residual_ref, basis_ref):
+def output_kernel(
+    gram_ref,
+    right_ref,
+    image_ref,
+    solution_out,
+    residual_out,
+    basis_out,
+    solution_ref,
+    residual_ref,
+    basis_ref,
+    sems,
+):
     def dot(a, b):
         return jnp.dot(a, b, precision=HIGH, preferred_element_type=F32)
 
@@ -519,6 +559,13 @@
         right = right_ref[:, part]
         solution_ref[:, part] = apply_step(right)
         residual_ref[:, part] = right - apply_step(image_ref[:, part])
+    copies = [
+        pltpu.make_async_copy(solution_ref, solution_out, sems.at[0]),
+        pltpu.make_async_copy(residual_ref, residual_out, sems.at[1]),
+        pltpu.make_async_copy(basis_ref, basis_out, sems.at[2]),
+    ]
+    copies[0].start()
+    copies[1].start()
 
     work = jnp.concatenate([new_gram, jnp.zeros((TR, 128 - TR), F32)], axis=1)
     work = jnp.where(lanes == rows + TR, 1.0, work)
@@ -538,6 +585,9 @@
     apply_lower = times((work * scale)[:, TR : 2 * TR])
     for part in parts:
         basis_ref[:, part] = apply_lower(residual_ref[:, part])
+    copies[2].start()
+    for copy in copies:
+        copy.wait()
 
 
 def per_device(
@@ -594,6 +644,7 @@
         out_specs=(vmem, vmem, vmem),
         scratch_shapes=[
             pltpu.VMEM((Q_ALL * (LO // 128) * TR, 128), F32),
+            pltpu.VMEM((Q_PRODUCT * 2 * TR, LO), BF16),
             pltpu.VMEM((2, 4 * NP, 4 * NP), BF16),
             pltpu.VMEM((chunks, LO, CHUNK), BF16),
             pltpu.VMEM((LO, 2 * F), BF16),
@@ -622,7 +673,8 @@
         output_kernel,
         out_shape=(out, out, out),
         in_specs=[vmem] * 3,
-        out_specs=(vmem, vmem, vmem),
+        out_specs=(pl.BlockSpec(memory_space=pl.ANY),) * 3,
+        scratch_shapes=[pltpu.VMEM((TR, NODE_DEV), F32)] * 3 + [pltpu.SemaphoreType.DMA((3,))],
         compiler_params=pltpu.CompilerParams(vmem_limit_bytes=61 * 2**20),
         name="output_stage",
     )(gram, right, image)

time: 77.1 us -> 68 us (0.88)
  Pallas kernels: 76.2 us -> 67.2 us
    pallas_call x1, Pallas kernels: 56.6 us -> 47.5 us  [per_device(): pl.pallas_call(functools.partial(exchange_kernel, n), out_shape=(field, f...]
where the time goes in v5:
time: 68 us; the launch traced here: 67.8 us
  Pallas kernels  67.2 us (99%)
    pallas_call x1, Pallas kernels, per_device(): pl.pallas_call(functools.partial(exchange_kernel, n), out_shape=(field, f...  47.5 us
    pallas_call x1, Pallas kernels, per_device(): pl.pallas_call(pair_kernel, out_shape=(jax.ShapeDtypeStruct((chunks, 2 *...  10.8 us
    pallas_call x1, Pallas kernels, per_device(): pl.pallas_call(output_kernel, out_shape=(out, out, out), in_specs=[vmem]...  8.81 us

profile of v5, /device:TPU:0, one launch (start us, length us, event | category | flops | bytes accessed | tf_op | source)
XLA Modules:
  0.0 67.8 jit_solution(14373488060840155247)
XLA Ops:
  0.6 10.8 %pair_stage.1 = (bf16[16,64,512]{2,1,0:T(8,128)(2,1)}, s32[16,512]{1,0:T(8,128)}, s32[16,512]{1,0:T(8,128)}, f32[16,512]{1,0:T(8,128)}, s32[2,768]{1,0:T(2,128)}, /*index=5*/s32[2,768]{1,0:T(2,128)}) custom-call(s32[256]{0:T(256)} %target_ref.1, s32[256]{0:T(256)} %source_ref.1, bf16[256,4096]{1,0:T(8,128)(2,1)} %blocks_hbm.1, bf16[32,8192]{1,0:T(8,128)(2,1)} %values_ref.1, ...), custom_call_target="tpu_custom_call" | custom-call | tf_op jit(solution)/shard_map/pair_stage/pallas_call | solution.py:604
  11.5 47.5 %exchange_stage.1 = (f32[32,3456]{1,0:T(8,128)}, f32[32,3456]{1,0:T(8,128)}, f32[32,128]{1,0:T(8,128)}) custom-call(bf16[16,64,512]{2,1,0:T(8,128)(2,1)} %get-tuple-element.12.sums_ref, s32[16,512]{1,0:T(8,128)} %get-tuple-element.13.lo_ref, s32[16,512]{1,0:T(8,128)} %get-tuple-element.14.q_ref, f32[16,512]{1,0:T(8,128)} %get-tuple-element.15.scale_ref, ...), custom_call_target="tpu_custom_call" | custom-call | tf_op jit(solution)/shard_map/exchange_stage/pallas_call | solution.py:640
  59.0 8.8 %output_stage.1 = (f32[32,3456]{1,0:T(8,128)}, f32[32,3456]{1,0:T(8,128)}, f32[32,3456]{1,0:T(8,128)}) custom-call(f32[32,128]{1,0:T(8,128)} %get-tuple-element.18.gram_ref, f32[32,3456]{1,0:T(8,128)} %get-tuple-element.19.right_ref, f32[32,3456]{1,0:T(8,128)} %get-tuple-element.20.image_ref), custom_call_target="tpu_custom_call" | custom-call | tf_op jit(solution)/shard_map/output_stage/pallas_call | solution.py:672

commit v6 on v5

--- a/solution.py
+++ b/solution.py
@@ -11,14 +11,14 @@
 NP = 64
 NODE_DEV = 3456
 F = 768
-LO = 384
-Q_OWN = NODE_DEV // LO
+LO = 256
+Q_OWN = -(-NODE_DEV // LO)
 Q_FACE = F // LO
 Q_ALL = Q_OWN + 2 * Q_FACE
 OWN = Q_OWN * TR
 FACE = Q_FACE * TR
 CHUNK = 512
-Q_PRODUCT = 5
+Q_PRODUCT = 7
 GROUP = 8
 MESH = pl.DeviceIdType.MESH
 HIGH = lax.Precision.HIGHEST
@@ -121,8 +121,8 @@
 
 
 def split_slots(slots):
-    q = jnp.right_shift(jnp.right_shift(slots, 7) * 43, 7)
-    return q, slots - q * LO
+    padded = jnp.where(slots < NODE_DEV, slots, slots + (Q_OWN * LO - NODE_DEV))
+    return jnp.right_shift(padded, 8), jnp.bitwise_and(padded, LO - 1)
 
 
 def pair_kernel(
@@ -372,6 +372,11 @@
 
         lax.fori_loop(0, chunks, step_sums, 0, unroll=2)
 
+    def write_out(ref, value):
+        for q in own_blocks:
+            end = min((q + 1) * LO, NODE_DEV)
+            ref[:, q * LO : end] = value[q * TR : (q + 1) * TR, 0 : end - q * LO]
+
     own_sums(sums_ref, 0)
     for way in range(2):
         face_hot[:, way * F : (way + 1) * F] = one_hot(face_lo_ref[way : way + 1, :])
@@ -393,8 +398,8 @@
     right = settle(ext[0, 0:OWN, :], 0)
     fill(0, right)
 
-    own_tiles, face_tiles = Q_OWN * LO // 128, 2 * F // 128
-    first_tile = Q_PRODUCT * LO // 128
+    own_tiles, face_tiles = NODE_DEV // 128, 2 * F // 128
+    first_tile, first_face = Q_PRODUCT * LO // 128, Q_OWN * LO // 128
 
     def own_gather(q_row, lo_row, marks):
         return gather(table, first_tile, own_tiles - first_tile, q_row, lo_row) + gather_product(
@@ -416,15 +421,14 @@
         return carry
 
     lax.fori_loop(0, chunks, own_values, 0, unroll=2)
-    for q in own_blocks:
-        right_ref[:, q * LO : (q + 1) * LO] = right[q * TR : (q + 1) * TR]
+    write_out(right_ref, right)
     for way in (1, 0):
         arrive(outgoing.at[way], 1, way)
         fill(Q_OWN if way else Q_OWN + Q_FACE, incoming[1, way])
 
     def face_values(step):
         q_row, lo_row = q_ref[pl.ds(step, 1), :], lo_ref[pl.ds(step, 1), :]
-        return gather(table, own_tiles, face_tiles, q_row, lo_row)
+        return gather(table, first_face, face_tiles, q_row, lo_row)
 
     def elements(step, from_faces):
         q_row = q_ref[pl.ds(step, 1), :]
@@ -453,8 +457,7 @@
     arrive(ext.at[1, down_rows], 2, 0)
     arrive(ext.at[1, up_rows], 2, 1)
     image = settle(ext[1, 0:OWN, :], 2)
-    for q in own_blocks:
-        image_ref[:, q * LO : (q + 1) * LO] = image[q * TR : (q + 1) * TR]
+    write_out(image_ref, image)
 
     stack = jnp.concatenate(
         [
@@ -553,7 +556,7 @@
 
         return apply
 
-    parts = [slice(at, at + 3 * LO) for at in range(0, Q_OWN * LO, 3 * LO)]
+    parts = [slice(at, at + NODE_DEV // 3) for at in range(0, NODE_DEV, NODE_DEV // 3)]
     apply_step = times(step)
     for part in parts:
         right = right_ref[:, part]

time: 68 us -> 65.4 us (0.962)
  Pallas kernels: 67.2 us -> 64.6 us
    pallas_call x1, Pallas kernels: 47.5 us -> 44.9 us  [per_device(): pl.pallas_call(functools.partial(exchange_kernel, n), out_shape=(field, f...]
where the time goes in v6:
time: 65.4 us; the launch traced here: 65.2 us
  Pallas kernels  64.6 us (99%)
    pallas_call x1, Pallas kernels, per_device(): pl.pallas_call(functools.partial(exchange_kernel, n), out_shape=(field, f...  44.9 us
    pallas_call x1, Pallas kernels, per_device(): pl.pallas_call(pair_kernel, out_shape=(jax.ShapeDtypeStruct((chunks, 2 *...  10.8 us
    pallas_call x1, Pallas kernels, per_device(): pl.pallas_call(output_kernel, out_shape=(out, out, out), in_specs=[vmem]...  8.81 us

profile of v6, /device:TPU:0, one launch (start us, length us, event | category | flops | bytes accessed | tf_op | source)
XLA Modules:
  0.0 65.2 jit_solution(9234867460700744735)
XLA Ops:
  0.6 10.8 %pair_stage.1 = (bf16[16,64,512]{2,1,0:T(8,128)(2,1)}, s32[16,512]{1,0:T(8,128)}, s32[16,512]{1,0:T(8,128)}, f32[16,512]{1,0:T(8,128)}, s32[2,768]{1,0:T(2,128)}, /*index=5*/s32[2,768]{1,0:T(2,128)}) custom-call(s32[256]{0:T(256)} %target_ref.1, s32[256]{0:T(256)} %source_ref.1, bf16[256,4096]{1,0:T(8,128)(2,1)} %blocks_hbm.1, bf16[32,8192]{1,0:T(8,128)(2,1)} %values_ref.1, ...), custom_call_target="tpu_custom_call" | custom-call | tf_op jit(solution)/shard_map/pair_stage/pallas_call | solution.py:607
  11.5 44.9 %exchange_stage.1 = (f32[32,3456]{1,0:T(8,128)}, f32[32,3456]{1,0:T(8,128)}, f32[32,128]{1,0:T(8,128)}) custom-call(bf16[16,64,512]{2,1,0:T(8,128)(2,1)} %get-tuple-element.12.sums_ref, s32[16,512]{1,0:T(8,128)} %get-tuple-element.13.lo_ref, s32[16,512]{1,0:T(8,128)} %get-tuple-element.14.q_ref, f32[16,512]{1,0:T(8,128)} %get-tuple-element.15.scale_ref, ...), custom_call_target="tpu_custom_call" | custom-call | tf_op jit(solution)/shard_map/exchange_stage/pallas_call | solution.py:643
  56.4 8.8 %output_stage.1 = (f32[32,3456]{1,0:T(8,128)}, f32[32,3456]{1,0:T(8,128)}, f32[32,3456]{1,0:T(8,128)}) custom-call(f32[32,128]{1,0:T(8,128)} %get-tuple-element.18.gram_ref, f32[32,3456]{1,0:T(8,128)} %get-tuple-element.19.right_ref, f32[32,3456]{1,0:T(8,128)} %get-tuple-element.20.image_ref), custom_call_target="tpu_custom_call" | custom-call | tf_op jit(solution)/shard_map/output_stage/pallas_call | solution.py:675

commit v7 on v6

--- a/solution.py
+++ b/solution.py
@@ -95,6 +95,13 @@
     return joined(add_up(spread(stack, q_row, blocks), hot))
 
 
+def scatter_two(values, q_ref, step, blocks, marks):
+    left = [
+        spread(values[2 * step + b], q_ref[pl.ds(2 * step + b, 1), :], blocks) for b in range(2)
+    ]
+    return joined(add_up(jnp.concatenate(left, axis=1), jnp.concatenate(marks, axis=1)))
+
+
 def gather(table, first_tile, tiles, q_row, lo_row):
     tile_row = q_row * (LO // 128) + jnp.right_shift(lo_row, 7)
     lane_row = jnp.bitwise_and(lo_row, 127)
@@ -142,6 +149,7 @@
     face_q_ref,
     blocks_ref,
     flat,
+    flat_two,
     table,
     total,
     wide,
@@ -203,31 +211,37 @@
     total[...] = jnp.zeros_like(total)
     fetch.wait()
 
-    def lay_out(g, carry):
+    rounds = pairs // 16
+
+    def lay_out(g, buffer):
         rows = blocks_ref[pl.ds(pl.multiple_of(g * 16, 16), 16), :]
         for c in range(32):
-            flat[pl.ds(g * 512 + c, 16, stride=32), :] = rows[:, c * 128 : (c + 1) * 128].astype(F32)
-        return carry
-
-    lax.fori_loop(0, pairs // 16, lay_out, 0)
-
-    def multiply(step, carry):
+            buffer[pl.ds(c, 16, stride=32), :] = rows[:, c * 128 : (c + 1) * 128].astype(F32)
+
+    def multiply(first, at, buffer):
         left, right = [], []
         for g in range(4):
-            p = step * 4 + g
-            left.append(table[source_ref[p]])
-            block = flat[pl.ds(pl.multiple_of(p * 32, 32), 32), :]
+            left.append(table[source_ref[first + at + g]])
+            block = buffer[(at + g) * 32 : (at + g + 1) * 32, :]
             right.append(jnp.where(lanes < 64, block, 0.0).astype(BF16))
             right.append(jnp.where(lanes < 64, 0.0, block).astype(BF16))
         product = add_up(jnp.concatenate(left, axis=0), jnp.concatenate(right, axis=0))
         for g in range(4):
             part = product[g * TR : (g + 1) * TR, (g // 2) * 128 : (g // 2 + 1) * 128]
             keep = (lanes < 64) if g % 2 == 0 else (lanes >= 64)
-            at = target_ref[step * 4 + g]
-            total[at] = total[at] + jnp.where(keep, part, 0.0)
+            to = target_ref[first + at + g]
+            total[to] = total[to] + jnp.where(keep, part, 0.0)
+
+    lay_out(0, flat)
+
+    def two_rounds(step, carry):
+        for now, here, later in ((2 * step, flat, flat_two), (2 * step + 1, flat_two, flat)):
+            lay_out(jnp.minimum(now + 1, rounds - 1), later)
+            for at in range(0, 16, 4):
+                multiply(now * 16, at, here)
         return carry
 
-    lax.fori_loop(0, pairs // 4, multiply, 0, unroll=8)
+    lax.fori_loop(0, rounds // 2, two_rounds, 0)
 
     def add(step, carry):
         tiles = []
@@ -343,12 +357,13 @@
                 )
 
     def face_sums(step, carry):
-        marks = one_hot(lo_ref[pl.ds(step, 1), :])
-        hot[step] = marks
-        ext[0, OWN:, :] += scatter(sums_ref[step], q_ref[pl.ds(step, 1), :], face_blocks, marks)
+        marks = [one_hot(lo_ref[pl.ds(2 * step + b, 1), :]) for b in range(2)]
+        for b in range(2):
+            hot[2 * step + b] = marks[b]
+        ext[0, OWN:, :] += scatter_two(sums_ref, q_ref, step, face_blocks, marks)
         return carry
 
-    lax.fori_loop(0, chunks, face_sums, 0, unroll=2)
+    lax.fori_loop(0, chunks // 2, face_sums, 0, unroll=2)
     partners = group + layers - 2
     crossing = jnp.logical_or(cross_up, cross_down)
 
@@ -365,12 +380,11 @@
 
     def own_sums(values, phase):
         def step_sums(step, carry):
-            ext[phase, 0:OWN, :] += scatter(
-                values[step], q_ref[pl.ds(step, 1), :], own_blocks, hot[step]
-            )
+            marks = [hot[2 * step + b] for b in range(2)]
+            ext[phase, 0:OWN, :] += scatter_two(values, q_ref, step, own_blocks, marks)
             return carry
 
-        lax.fori_loop(0, chunks, step_sums, 0, unroll=2)
+        lax.fori_loop(0, chunks // 2, step_sums, 0, unroll=2)
 
     def write_out(ref, value):
         for q in own_blocks:
@@ -618,7 +632,8 @@
         out_specs=(vmem,) * 6,
         scratch_shapes=[
             pltpu.VMEM(pair_blocks.shape, BF16),
-            pltpu.VMEM((pairs * 32, 128), F32),
+            pltpu.VMEM((16 * 32, 128), F32),
+            pltpu.VMEM((16 * 32, 128), F32),
             pltpu.VMEM((elements, TR, 128), BF16),
             pltpu.VMEM((elements, TR, 128), F32),
             pltpu.VMEM((elements, 128), F32),

time: 65.4 us -> 61.9 us (0.946)
  Pallas kernels: 64.6 us -> 61 us
    pallas_call x1, Pallas kernels: 44.9 us -> 42.6 us  [per_device(): pl.pallas_call(functools.partial(exchange_kernel, n), out_shape=(field, f...]
    pallas_call x1, Pallas kernels: 10.8 us -> 9.66 us  [per_device(): pl.pallas_call(pair_kernel, out_shape=(jax.ShapeDtypeStruct((chunks, 2 *...]
where the time goes in v7:
time: 61.9 us; the launch traced here: 61.7 us
  Pallas kernels  61 us (99%)
  between operations  0.65 us (1%)
    pallas_call x1, Pallas kernels, per_device(): pl.pallas_call(functools.partial(exchange_kernel, n), out_shape=(field, f...  42.6 us
    pallas_call x1, Pallas kernels, per_device(): pl.pallas_call(pair_kernel, out_shape=(jax.ShapeDtypeStruct((chunks, 2 *...  9.66 us
    pallas_call x1, Pallas kernels, per_device(): pl.pallas_call(output_kernel, out_shape=(out, out, out), in_specs=[vmem]...  8.81 us

profile of v7, /device:TPU:0, one launch (start us, length us, event | category | flops | bytes accessed | tf_op | source)
XLA Modules:
  0.0 61.7 jit_solution(16757150140363429005)
XLA Ops:
  0.6 9.7 %pair_stage.1 = (bf16[16,64,512]{2,1,0:T(8,128)(2,1)}, s32[16,512]{1,0:T(8,128)}, s32[16,512]{1,0:T(8,128)}, f32[16,512]{1,0:T(8,128)}, s32[2,768]{1,0:T(2,128)}, /*index=5*/s32[2,768]{1,0:T(2,128)}) custom-call(s32[256]{0:T(256)} %target_ref.1, s32[256]{0:T(256)} %source_ref.1, bf16[256,4096]{1,0:T(8,128)(2,1)} %blocks_hbm.1, bf16[32,8192]{1,0:T(8,128)(2,1)} %values_ref.1, ...), custom_call_target="tpu_custom_call" | custom-call | tf_op jit(solution)/shard_map/pair_stage/pallas_call | solution.py:621
  10.3 42.6 %exchange_stage.1 = (f32[32,3456]{1,0:T(8,128)}, f32[32,3456]{1,0:T(8,128)}, f32[32,128]{1,0:T(8,128)}) custom-call(bf16[16,64,512]{2,1,0:T(8,128)(2,1)} %get-tuple-element.12.sums_ref, s32[16,512]{1,0:T(8,128)} %get-tuple-element.13.lo_ref, s32[16,512]{1,0:T(8,128)} %get-tuple-element.14.q_ref, f32[16,512]{1,0:T(8,128)} %get-tuple-element.15.scale_ref, ...), custom_call_target="tpu_custom_call" | custom-call | tf_op jit(solution)/shard_map/exchange_stage/pallas_call | solution.py:658
  52.9 8.8 %output_stage.1 = (f32[32,3456]{1,0:T(8,128)}, f32[32,3456]{1,0:T(8,128)}, f32[32,3456]{1,0:T(8,128)}) custom-call(f32[32,128]{1,0:T(8,128)} %get-tuple-element.18.gram_ref, f32[32,3456]{1,0:T(8,128)} %get-tuple-element.19.right_ref, f32[32,3456]{1,0:T(8,128)} %get-tuple-element.20.image_ref), custom_call_target="tpu_custom_call" | custom-call | tf_op jit(solution)/shard_map/output_stage/pallas_call | solution.py:690

commit v8 on v7

--- a/solution.py
+++ b/solution.py
@@ -95,9 +95,9 @@
     return joined(add_up(spread(stack, q_row, blocks), hot))
 
 
-def scatter_two(values, q_ref, step, blocks, marks):
+def scatter_four(values, q_ref, step, blocks, marks):
     left = [
-        spread(values[2 * step + b], q_ref[pl.ds(2 * step + b, 1), :], blocks) for b in range(2)
+        spread(values[4 * step + b], q_ref[pl.ds(4 * step + b, 1), :], blocks) for b in range(4)
     ]
     return joined(add_up(jnp.concatenate(left, axis=1), jnp.concatenate(marks, axis=1)))
 
@@ -357,13 +357,13 @@
                 )
 
     def face_sums(step, carry):
-        marks = [one_hot(lo_ref[pl.ds(2 * step + b, 1), :]) for b in range(2)]
-        for b in range(2):
-            hot[2 * step + b] = marks[b]
-        ext[0, OWN:, :] += scatter_two(sums_ref, q_ref, step, face_blocks, marks)
+        marks = [one_hot(lo_ref[pl.ds(4 * step + b, 1), :]) for b in range(4)]
+        for b in range(4):
+            hot[4 * step + b] = marks[b]
+        ext[0, OWN:, :] += scatter_four(sums_ref, q_ref, step, face_blocks, marks)
         return carry
 
-    lax.fori_loop(0, chunks // 2, face_sums, 0, unroll=2)
+    lax.fori_loop(0, chunks // 4, face_sums, 0)
     partners = group + layers - 2
     crossing = jnp.logical_or(cross_up, cross_down)
 
@@ -380,11 +380,11 @@
 
     def own_sums(values, phase):
         def step_sums(step, carry):
-            marks = [hot[2 * step + b] for b in range(2)]
-            ext[phase, 0:OWN, :] += scatter_two(values, q_ref, step, own_blocks, marks)
+            marks = [hot[4 * step + b] for b in range(4)]
+            ext[phase, 0:OWN, :] += scatter_four(values, q_ref, step, own_blocks, marks)
             return carry
 
-        lax.fori_loop(0, chunks // 2, step_sums, 0, unroll=2)
+        lax.fori_loop(0, chunks // 4, step_sums, 0)
 
     def write_out(ref, value):
         for q in own_blocks:

time: 61.9 us -> 61.9 us (level)
  no operation moved by 1% of the time
where the time goes in v8:
time: 61.9 us; the launch traced here: 61.7 us
  Pallas kernels  61 us (99%)
  between operations  0.65 us (1%)
    pallas_call x1, Pallas kernels, per_device(): pl.pallas_call(functools.partial(exchange_kernel, n), out_shape=(field, f...  42.6 us
    pallas_call x1, Pallas kernels, per_device(): pl.pallas_call(pair_kernel, out_shape=(jax.ShapeDtypeStruct((chunks, 2 *...  9.63 us
    pallas_call x1, Pallas kernels, per_device(): pl.pallas_call(output_kernel, out_shape=(out, out, out), in_specs=[vmem]...  8.81 us

profile of v8, /device:TPU:0, one launch (start us, length us, event | category | flops | bytes accessed | tf_op | source)
XLA Modules:
  0.0 61.7 jit_solution(10004115709845455283)
XLA Ops:
  0.6 9.6 %pair_stage.1 = (bf16[16,64,512]{2,1,0:T(8,128)(2,1)}, s32[16,512]{1,0:T(8,128)}, s32[16,512]{1,0:T(8,128)}, f32[16,512]{1,0:T(8,128)}, s32[2,768]{1,0:T(2,128)}, /*index=5*/s32[2,768]{1,0:T(2,128)}) custom-call(s32[256]{0:T(256)} %target_ref.1, s32[256]{0:T(256)} %source_ref.1, bf16[256,4096]{1,0:T(8,128)(2,1)} %blocks_hbm.1, bf16[32,8192]{1,0:T(8,128)(2,1)} %values_ref.1, ...), custom_call_target="tpu_custom_call" | custom-call | tf_op jit(solution)/shard_map/pair_stage/pallas_call | solution.py:621
  10.3 42.6 %exchange_stage.1 = (f32[32,3456]{1,0:T(8,128)}, f32[32,3456]{1,0:T(8,128)}, f32[32,128]{1,0:T(8,128)}) custom-call(bf16[16,64,512]{2,1,0:T(8,128)(2,1)} %get-tuple-element.12.sums_ref, s32[16,512]{1,0:T(8,128)} %get-tuple-element.13.lo_ref, s32[16,512]{1,0:T(8,128)} %get-tuple-element.14.q_ref, f32[16,512]{1,0:T(8,128)} %get-tuple-element.15.scale_ref, ...), custom_call_target="tpu_custom_call" | custom-call | tf_op jit(solution)/shard_map/exchange_stage/pallas_call | solution.py:658
  52.9 8.8 %output_stage.1 = (f32[32,3456]{1,0:T(8,128)}, f32[32,3456]{1,0:T(8,128)}, f32[32,3456]{1,0:T(8,128)}) custom-call(f32[32,128]{1,0:T(8,128)} %get-tuple-element.18.gram_ref, f32[32,3456]{1,0:T(8,128)} %get-tuple-element.19.right_ref, f32[32,3456]{1,0:T(8,128)} %get-tuple-element.20.image_ref), custom_call_target="tpu_custom_call" | custom-call | tf_op jit(solution)/shard_map/output_stage/pallas_call | solution.py:690
